TPU v7x, 256 devices: a whole 4x4x8 slice. The times are simulated.
256 devices in a mesh: gx: 64 (over z, y, core), gy: 4 (over x).
Axes of the slice: x: 4, y: 4, z: 8, core: 2. Of those that a mesh axis runs over, the one named last changes fastest.
Arguments:
- hamiltonian: float32 [64, 4, 4, 64, 512], P('gx', 'gy')
- intersection: float32 [64, 4, 4, 64, 512], P('gx', 'gy')
- density: float32 [64, 4, 4, 64, 512], P('gx', 'gy')
- leaving: int32 [64, 4, 4, 1], P('gx', 'gy'), may hold values from 0 to 3, as said below
- code_ids: int32 [64, 4, 4, 8], P('gx', 'gy'), may hold values from 0 to 8, as said below
- slot_ids: int32 [64, 4, 4, 8], P('gx', 'gy'), may hold values from 0 to 3, as said below
Outputs:
- purified: float32 [64, 4, 4, 64, 512], P('gx', 'gy')
- energy: float32 [], replicated
Inputs may be any that keep to these rules, and one draw needn't show every extreme that they name: `leaving`: the slots listed for one device are all different. `code_ids`: the first entry of every block row is code 4 with the row's own slot; the 8 (code, slot) pairs of a row are all different. `slot_ids`: paired with code_ids as stated there.
All inputs are finite; a program needn't handle non-finite values.
Results may differ from a plain program's by a relative error of at most 0.0003.
Values sent between devices are 32-bit elements; how exact they have to be, the bound alone decides.
A program may use at most 128 MiB of HBM per device.

v0:
```python
import jax
import jax.numpy as jnp
from jax import lax
from jax.sharding import PartitionSpec as P

ITERS = 2


def passed_along(block, axis, distance):
    devices = range(lax.axis_size(axis))
    route = [((i - distance) % len(devices), i) for i in devices]
    return lax.ppermute(block, axis, route)


def with_halo(block, sides, width):
    for axis, dim in sides:
        count = lax.axis_size(axis)
        forward = [(i, i + 1) for i in range(count - 1)]
        forward.append((count - 1, 0))
        backward = [(target, source) for source, target in forward]
        low = lax.ppermute(
            lax.slice_in_dim(block, block.shape[dim] - width, None, axis=dim), axis, forward
        )
        high = lax.ppermute(lax.slice_in_dim(block, 0, width, axis=dim), axis, backward)
        block = jnp.concatenate([low, block, high], axis=dim)
    return block


def local_product(left_rows, rim_rows, code_list, slot_list, rim_codes, rim_slots):
    groups, width, columns = left_rows.shape
    kept = code_list.shape[1]
    row_index = code_list * groups + slot_list
    next_codes = jnp.take(rim_codes.reshape(9 * groups, kept), row_index, axis=0)
    next_slots = jnp.take(rim_slots.reshape(9 * groups, kept), row_index, axis=0)
    left_dx = code_list // 3 - 1
    left_dy = code_list % 3 - 1
    next_dx = next_codes // 3 - 1
    next_dy = next_codes % 3 - 1
    same_x = left_dx[:, :, None, None] + next_dx[:, :, None, :] == left_dx[:, None, :, None]
    same_y = left_dy[:, :, None, None] + next_dy[:, :, None, :] == left_dy[:, None, :, None]
    same_slot = next_slots[:, :, None, :] == slot_list[:, None, :, None]
    matches = (same_x & same_y & same_slot).astype(jnp.float32)
    gathered = jnp.take(rim_rows.reshape(9 * groups, width, columns), row_index.reshape(-1), axis=0)
    gathered = gathered.reshape(groups, kept, width, kept, width)
    partial_rows = jnp.einsum(
        "ipar,iarcq->iapcq",
        left_rows.reshape(groups, width, kept, width),
        gathered,
        precision=lax.Precision.HIGHEST,
    )
    result = jnp.einsum("iabc,iapcq->ipbq", matches, partial_rows, precision=lax.Precision.HIGHEST)
    return result.reshape(groups, width, kept * width)


def cross_x(moving_rows, offset):
    return passed_along(moving_rows, "gx", offset)


def cross_y(moving_rows, offset):
    return passed_along(moving_rows, "gy", offset)


def neighbourhood(rows_here):
    lifted = rows_here[None, None]
    whole = with_halo(lifted, (("gx", 0), ("gy", 1)), 1)
    return whole.reshape((9,) + rows_here.shape)


def global_count(value):
    return lax.psum(value, ("gx", "gy"))


def shards(hamiltonian, intersection, density, leaving, code_ids, slot_ids):
    stacked = jnp.stack([hamiltonian[0, 0], intersection[0, 0], density[0, 0]])
    depart = leaving[0, 0]
    arrive = jnp.concatenate(
        [
            cross_x(stacked[:, depart[0]], 1),
            cross_x(stacked[:, depart[1]], -1),
            cross_y(stacked[:, depart[2]], 1),
            cross_y(stacked[:, depart[3]], -1),
        ],
        axis=1,
    )
    landing = jnp.concatenate([depart[1], depart[0], depart[3], depart[2]])
    stacked = stacked.at[:, landing].set(arrive)
    ham_rows = stacked[0]
    ovl_rows = stacked[1]
    den_rows = stacked[2]
    code_list = code_ids[0, 0]
    slot_list = slot_ids[0, 0]
    pattern = jnp.stack([code_list, slot_list])[None, None]
    pattern_all = with_halo(pattern, (("gx", 0), ("gy", 1)), 1)
    groups, kept = code_list.shape
    rim_codes = pattern_all[:, :, 0].reshape(9, groups, kept)
    rim_slots = pattern_all[:, :, 1].reshape(9, groups, kept)

    def times(left_rows, rim_rows):
        return local_product(left_rows, rim_rows, code_list, slot_list, rim_codes, rim_slots)

    ovl_rim = neighbourhood(ovl_rows)
    count_start = global_count(jnp.sum(den_rows * ovl_rows))
    mixed = den_rows
    for step in range(ITERS):
        den_rim = neighbourhood(den_rows)
        first = times(den_rows, ovl_rim)
        second = times(first, den_rim)
        third = times(second, ovl_rim)
        fourth = times(third, den_rim)
        mixed = 3.0 * second - 2.0 * fourth
        if step + 1 < ITERS:
            den_rows = count_start / global_count(jnp.sum(mixed * ovl_rows)) * mixed
    basis_total = mixed.shape[0] * mixed.shape[1] * lax.axis_size("gx") * lax.axis_size("gy")
    scale_last = count_start / lax.psum(jnp.sum(mixed * ovl_rows), ("gx", "gy"))
    den_rows = scale_last * mixed
    energy = lax.psum(jnp.sum(den_rows * ham_rows), ("gx", "gy")) / jnp.float32(basis_total)
    return (den_rows[None, None], energy)


def solution(mesh):
    placed = (
        P("gx", "gy", None, None, None),
        P("gx", "gy", None, None, None),
        P("gx", "gy", None, None, None),
        P("gx", "gy", None, None),
        P("gx", "gy", None, None),
        P("gx", "gy", None, None),
    )
    return jax.shard_map(
        shards,
        mesh=mesh,
        in_specs=placed,
        out_specs=(P("gx", "gy", None, None, None), P()),
        check_vma=False,
    )
```

profile of v0, /device:TPU:1, one launch (start us, length us, event | category | flops | bytes accessed | tf_op | source)
XLA Modules:
  0.0 593.5 jit_solution(3605249791912820819)
XLA Ops:
  0.7 1.5 fusion.104
  9.8 1.5 pad_maximum_fusion.3
  11.5 2.8 collective-permute-start
  14.3 1.2 collective-permute-start.2
  15.5 2.4 collective-permute-start.3
  17.9 6.1 %collective-permute-start.9 = (s32[1,1,2,4,8]{4,3,2,1,0:T(4,128)S(1)}, s32[1,1,2,4,8]{4,3,2,1,0:T(4,128)S(1)}, u32[]{:S(2)}, u32[]{:S(2)}) collective-permute-start(s32[1,1,2,4,8]{4,3,2,1,0:T(4,128)S(1)} %add_bitcast_fusion), channel_id=1, source_target_pairs={{4,0},{8,4},{12,8},{16,12},{20,16},{24,20},{28,24},{32,28},{36,32}... | collective-permute-start | bytes 776 | tf_op jit(solution)/shard_map/ppermute | solution.py:24
  24.0 2.6 fusion.101
  26.7 0.9 scatter_fusion
  27.9 3.4 collective-permute-start.5
  31.3 2.8 collective-permute-start.13
  34.2 2.5 collective-permute-done.5
  36.7 0.7 collective-permute-done.4
  37.4 2.5 pad_maximum_fusion.4
  39.9 2.7 collective-permute-start.7
  42.6 2.9 collective-permute-start.8
  45.6 1.4 pad_maximum_fusion.5
  47.0 2.9 collective-permute-start.15
  49.9 2.0 collective-permute-done.8
  52.0 3.1 collective-permute-start.11
  55.1 47.0 %collective-permute-done.11 = s32[3,1,2,4,8]{4,3,2,1,0:T(4,128)S(1)} collective-permute-done((s32[3,1,2,4,8]{4,3,2,1,0:T(4,128)S(1)}, s32[3,1,2,4,8]{4,3,2,1,0:T(4,128)S(1)}, u32[]{:S(2)}, u32[]{:S(2)}) %collective-permute-start.11) | collective-permute-done | bytes 800 | tf_op jit(solution)/shard_map/ppermute | solution.py:24
  102.6 4.7 collective-permute-done.10
  108.8 1.2 reshape_squeeze.3
  110.0 4.0 pad_maximum_fusion
  114.0 5.2 gather_fusion
  119.2 3.8 pad_maximum_fusion.1
  123.0 5.1 gather_fusion.3
  128.1 8.7 %broadcast_select_fusion.2 = (f32[32,64,512]{2,1,0:T(8,128)}, f32[32,64,512]{2,1,0:T(8,128)}) fusion(f32[32,64,512]{2,1,0:T(8,128)} %gather_fusion, pred[32]{0:T(512)(128)(4,1)S(1)} %compare_and_fusion.2, f32[32,64,512]{2,1,0:T(8,128)} %gather_fusion.3), kind=kLoop, calls=%fused_computation.43 | loop fusion | flops 2097152 | bytes 16777248 | tf_op jit(solution)/shard_map/jit(_take)/select_n | solution.py:43
  136.8 7.1 %reshape.364 = f32[4,8,64,8,64]{4,3,2,1,0:T(8,128)} reshape(f32[32,64,512]{2,1,0:T(8,128)} %get-tuple-element.68) | data formatting | bytes 8388608 | tf_op jit(solution)/shard_map/reshape | solution.py:44
  143.9 7.1 %reshape.365 = f32[4,8,64,8,64]{4,3,2,1,0:T(8,128)} reshape(f32[32,64,512]{2,1,0:T(8,128)} %get-tuple-element.69) | data formatting | bytes 8388608 | tf_op jit(solution)/shard_map/reshape | solution.py:44
  151.0 13.1 %fusion.30 = f32[4,8,64,8,64]{4,2,3,1,0:T(8,128)S(1)} fusion(f32[4,8,64,8,64]{4,3,2,1,0:T(8,128)} %reshape.364, f32[4,64,8,64,1]{3,2,1,0,4:T(8,128)S(1)} %bitcast.226), kind=kOutput, calls=%fused_computation.36 | convolution fusion | flops 805306368 | bytes 8912896 | tf_op jit(solution)/shard_map/ipar,iarcq->iapcq/dot_general | solution.py:45
  164.1 7.5 %fusion.32 = f32[4,64,8,64,1]{3,2,1,0,4:T(8,128)S(1)} fusion(f32[4,8,64,8,64]{4,2,3,1,0:T(8,128)S(1)} %fusion.30, pred[4,8,8,8]{3,2,1,0:T(8,128)(4,1)S(1)} %compare_and_fusion), kind=kOutput, calls=%fused_computation.48 | convolution fusion | flops 100663296 | bytes 4720640 | tf_op jit(solution)/shard_map/iabc,iapcq->ipbq/dot_general | solution.py:51
  171.7 9.3 %fusion.22 = f32[4,8,64,8,64]{4,2,3,1,0:T(8,128)S(1)} fusion(f32[4,8,64,8,64]{4,3,2,1,0:T(8,128)S(1)} %copy-done, f32[4,64,8,64,1]{3,2,1,0,4:T(8,128)S(1)} %fusion.32), kind=kOutput, calls=%fused_computation.28 | convolution fusion | flops 805306368 | bytes 8912896 | tf_op jit(solution)/shard_map/ipar,iarcq->iapcq/dot_general | solution.py:45
  181.0 7.7 %fusion.12 = f32[4,64,64,8,1]{2,3,4,1,0:T(8,128)S(1)} fusion(f32[4,8,64,8,64]{4,2,3,1,0:T(8,128)S(1)} %fusion.22, pred[4,8,8,8]{3,2,1,0:T(8,128)(4,1)S(1)} %compare_and_fusion), kind=kOutput, calls=%fused_computation.18 | convolution fusion | flops 100663296 | bytes 4720640 | tf_op jit(solution)/shard_map/iabc,iapcq->ipbq/dot_general | solution.py:51
  188.7 8.9 %fusion.28 = f32[4,8,64,8,64]{4,2,3,1,0:T(8,128)S(1)} fusion(f32[4,8,64,8,64]{4,3,2,1,0:T(8,128)S(1)} %bitcast.218, f32[4,64,8,64,1]{3,2,1,0,4:T(8,128)S(1)} %bitcast.225), kind=kOutput, calls=%fused_computation.34 | convolution fusion | flops 805306368 | bytes 8912896 | tf_op jit(solution)/shard_map/ipar,iarcq->iapcq/dot_general | solution.py:45
  197.7 7.9 %fusion.35 = f32[4,64,8,64,1]{3,2,1,0,4:T(8,128)S(1)} fusion(f32[4,8,64,8,64]{4,2,3,1,0:T(8,128)S(1)} %fusion.28, pred[4,8,8,8]{3,2,1,0:T(8,128)(4,1)S(1)} %compare_and_fusion), kind=kOutput, calls=%fused_computation.49 | convolution fusion | flops 100663296 | bytes 4720640 | tf_op jit(solution)/shard_map/iabc,iapcq->ipbq/dot_general | solution.py:51
  205.6 9.1 %fusion.20 = f32[4,8,64,8,64]{4,2,3,1,0:T(8,128)S(1)} fusion(f32[4,8,64,8,64]{4,3,2,1,0:T(8,128)S(1)} %copy-done, f32[4,64,8,64,1]{3,2,1,0,4:T(8,128)S(1)} %fusion.35), kind=kOutput, calls=%fused_computation.26 | convolution fusion | flops 805306368 | bytes 8912896 | tf_op jit(solution)/shard_map/ipar,iarcq->iapcq/dot_general | solution.py:45
  214.7 7.6 %fusion.65 = f32[4,64,8,64]{3,2,1,0:T(8,128)S(1)} fusion(f32[4,8,64,8,64]{4,2,3,1,0:T(8,128)S(1)} %fusion.20, f32[4,64,64,8,1]{2,3,4,1,0:T(8,128)S(1)} %copy-done.2, pred[4,8,8,8]{3,2,1,0:T(8,128)(4,1)S(1)} %compare_and_fusion), kind=kOutput, calls=%fused_computation.59 | convolution fusion | flops 101056512 | bytes 5244928 | tf_op jit(solution)/shard_map/iabc,iapcq->ipbq/dot_general | solution.py:51
  222.6 0.9 fusion.79
  223.4 86.8 %all-reduce = (f32[]{:T(128)}, f32[]{:T(128)}) all-reduce(f32[]{:T(128)} %get-tuple-element.49, f32[]{:T(128)} %get-tuple-element.48), channel_id=1, replica_groups=mesh['gx'=64,'gy'=4] {'gx','gy'}, use_global_device_ids=true, to_apply=%region_2.0 | all-reduce | flops 2 | bytes 16 | tf_op jit(solution)/shard_map/psum | solution.py:70
  311.6 1.1 broadcast_multiply_fusion.1
  312.7 1.5 mul.132
  314.2 0.6 collective-permute-start.16
  315.1 5.9 collective-permute-done.16
  321.0 2.7 collective-permute-done.17
  323.8 1.8 collective-permute-start.19
  325.7 13.2 %fusion.26 = f32[4,8,64,8,64]{4,2,3,1,0:T(8,128)S(1)} fusion(f32[4,8,64,8,64]{4,3,2,1,0:T(8,128)} %reshape.364, f32[4,64,8,64,1]{3,2,1,0,4:T(8,128)S(1)} %fusion.105), kind=kOutput, calls=%fused_computation.32 | convolution fusion | flops 805306368 | bytes 8912896 | tf_op jit(solution)/shard_map/ipar,iarcq->iapcq/dot_general | solution.py:45
  338.8 7.5 %fusion.41 = f32[4,64,8,64,1]{3,2,1,0,4:T(8,128)S(1)} fusion(f32[4,8,64,8,64]{4,2,3,1,0:T(8,128)S(1)} %fusion.26, pred[4,8,8,8]{3,2,1,0:T(8,128)(4,1)S(1)} %compare_and_fusion), kind=kOutput, calls=%fused_computation.51 | convolution fusion | flops 100663296 | bytes 4720640 | tf_op jit(solution)/shard_map/iabc,iapcq->ipbq/dot_general | solution.py:51
  346.3 10.4 %collective-permute-done.19 = f32[3,1,4,64,512]{4,3,2,1,0:T(8,128)S(1)} collective-permute-done((f32[3,1,4,64,512]{4,3,2,1,0:T(8,128)S(1)}, f32[3,1,4,64,512]{4,3,2,1,0:T(8,128)S(1)}, u32[]{:S(2)}, u32[]{:S(2)}) %collective-permute-start.19) | collective-permute-done | bytes 1572896 | tf_op jit(solution)/shard_map/ppermute | solution.py:24
  356.7 2.7 collective-permute-done.18
  359.4 2.8 pad_maximum_fusion.2
  362.1 5.1 gather_fusion.4
  367.2 5.0 broadcast_select_fusion
  372.2 7.0 %reshape.366 = f32[4,8,64,8,64]{4,3,2,1,0:T(8,128)} reshape(f32[32,64,512]{2,1,0:T(8,128)} %broadcast_select_fusion) | data formatting | bytes 8388608 | tf_op jit(solution)/shard_map/reshape | solution.py:44
  379.2 12.9 %fusion.18 = f32[4,8,64,8,64]{4,2,3,1,0:T(8,128)S(1)} fusion(f32[4,8,64,8,64]{4,3,2,1,0:T(8,128)} %reshape.366, f32[4,64,8,64,1]{3,2,1,0,4:T(8,128)S(1)} %fusion.41), kind=kOutput, calls=%fused_computation.24 | convolution fusion | flops 805306368 | bytes 8912896 | tf_op jit(solution)/shard_map/ipar,iarcq->iapcq/dot_general | solution.py:45
  392.1 7.5 %fusion.4 = f32[4,64,64,8,1]{2,3,4,1,0:T(8,128)S(1)} fusion(f32[4,8,64,8,64]{4,2,3,1,0:T(8,128)S(1)} %fusion.18, pred[4,8,8,8]{3,2,1,0:T(8,128)(4,1)S(1)} %compare_and_fusion), kind=kOutput, calls=%fused_computation.10 | convolution fusion | flops 100663296 | bytes 4720640 | tf_op jit(solution)/shard_map/iabc,iapcq->ipbq/dot_general | solution.py:51
  399.7 13.4 %fusion.24 = f32[4,8,64,8,64]{4,2,3,1,0:T(8,128)S(1)} fusion(f32[4,8,64,8,64]{4,3,2,1,0:T(8,128)} %reshape.364, f32[4,64,8,64,1]{3,2,1,0,4:T(8,128)S(1)} %bitcast.224), kind=kOutput, calls=%fused_computation.30 | convolution fusion | flops 805306368 | bytes 8912896 | tf_op jit(solution)/shard_map/ipar,iarcq->iapcq/dot_general | solution.py:45
  413.0 7.5 %fusion.44 = f32[4,64,8,64,1]{3,2,1,0,4:T(8,128)S(1)} fusion(f32[4,8,64,8,64]{4,2,3,1,0:T(8,128)S(1)} %fusion.24, pred[4,8,8,8]{3,2,1,0:T(8,128)(4,1)S(1)} %compare_and_fusion), kind=kOutput, calls=%fused_computation.52 | convolution fusion | flops 100663296 | bytes 4720640 | tf_op jit(solution)/shard_map/iabc,iapcq->ipbq/dot_general | solution.py:51
  420.6 9.1 %fusion.16 = f32[4,8,64,8,64]{4,2,3,1,0:T(8,128)S(1)} fusion(f32[4,8,64,8,64]{4,3,2,1,0:T(8,128)S(1)} %bitcast.220, f32[4,64,8,64,1]{3,2,1,0,4:T(8,128)S(1)} %fusion.44), kind=kOutput, calls=%fused_computation.22 | convolution fusion | flops 805306368 | bytes 8912896 | tf_op jit(solution)/shard_map/ipar,iarcq->iapcq/dot_general | solution.py:45
  429.7 7.8 %fusion.56 = f32[4,64,8,64]{3,2,1,0:T(8,128)S(1)} fusion(f32[4,8,64,8,64]{4,2,3,1,0:T(8,128)S(1)} %fusion.16, f32[4,64,64,8,1]{2,3,4,1,0:T(8,128)S(1)} %fusion.4, pred[4,8,8,8]{3,2,1,0:T(8,128)(4,1)S(1)} %compare_and_fusion), kind=kOutput, calls=%fused_computation.56 | convolution fusion | flops 101056512 | bytes 5244928 | tf_op jit(solution)/shard_map/iabc,iapcq->ipbq/dot_general | solution.py:51
  437.8 0.7 fusion.80
  438.5 75.5 %psum.30 = f32[]{:T(128)} all-reduce(f32[]{:T(128)} %fusion.80), channel_id=1, replica_groups=mesh['gx'=64,'gy'=4] {'gx','gy'}, use_global_device_ids=true, to_apply=%region_6.9 | all-reduce | flops 1 | bytes 8 | tf_op jit(solution)/shard_map/psum | solution.py:114
  515.3 0.7 fusion.77
  516.1 74.3 %psum.31 = f32[]{:T(128)} all-reduce(f32[]{:T(128)} %fusion.77), channel_id=1, replica_groups=mesh['gx'=64,'gy'=4] {'gx','gy'}, use_global_device_ids=true, to_apply=%region_8.11 | all-reduce | flops 1 | bytes 8 | tf_op jit(solution)/shard_map/psum | solution.py:116
  590.4 1.1 mul.139
  (78 shorter events, 3.8 us)
Async XLA Ops:
  0.6 17.2 %copy-start.8 = (s32[1,1,4,8]{3,2,1,0:T(4,128)S(1)}, s32[1,1,4,8]{3,2,1,0:T(4,128)}, u32[]{:S(2)}) copy-start(s32[1,1,4,8]{3,2,1,0:T(4,128)} %param.14) | copy-start | bytes 388
  0.6 17.2 %copy-start.9 = (s32[1,1,4,8]{3,2,1,0:T(4,128)S(1)}, s32[1,1,4,8]{3,2,1,0:T(4,128)}, u32[]{:S(2)}) copy-start(s32[1,1,4,8]{3,2,1,0:T(4,128)} %param.15) | copy-start | bytes 388
  11.5 15.1 %collective-permute-start = (f32[3,1,64,512]{3,2,0,1:T(8,128)S(1)}, f32[3,1,64,512]{3,2,0,1:T(8,128)S(1)}, u32[]{:S(2)}, u32[]{:S(2)}) collective-permute-start(f32[3,1,64,512]{3,2,0,1:T(8,128)S(1)} %get-tuple-element.57), channel_id=1, source_target_pairs={{252,0},{0,4},{4,8},{8,12},{12,16},{16,20},{20,24},{24,28},{28,32}... | collective-permute-start | bytes 1179656 | tf_op jit(solution)/shard_map/ppermute | solution.py:12
  14.3 12.3 %collective-permute-start.2 = (f32[3,1,64,512]{3,2,0,1:T(8,128)S(1)}, f32[3,1,64,512]{3,2,0,1:T(8,128)S(1)}, u32[]{:S(2)}, u32[]{:S(2)}) collective-permute-start(f32[3,1,64,512]{3,2,0,1:T(8,128)S(1)} %get-tuple-element.58), channel_id=1, source_target_pairs={{3,0},{0,1},{1,2},{2,3},{7,4},{4,5},{5,6},{6,7},{11,8},{8,9},{9,10... | collective-permute-start | bytes 1179656 | tf_op jit(solution)/shard_map/ppermute | solution.py:12
  15.5 11.1 %collective-permute-start.1 = (f32[3,1,64,512]{3,2,0,1:T(8,128)S(1)}, f32[3,1,64,512]{3,2,0,1:T(8,128)S(1)}, u32[]{:S(2)}, u32[]{:S(2)}) collective-permute-start(f32[3,1,64,512]{3,2,0,1:T(8,128)S(1)} %get-tuple-element.59), channel_id=1, source_target_pairs={{4,0},{8,4},{12,8},{16,12},{20,16},{24,20},{28,24},{32,28},{36,32}... | collective-permute-start | bytes 1179656 | tf_op jit(solution)/shard_map/ppermute | solution.py:12
  15.5 11.1 %collective-permute-start.3 = (f32[3,1,64,512]{3,2,0,1:T(8,128)S(1)}, f32[3,1,64,512]{3,2,0,1:T(8,128)S(1)}, u32[]{:S(2)}, u32[]{:S(2)}) collective-permute-start(f32[3,1,64,512]{3,2,0,1:T(8,128)S(1)} %get-tuple-element.60), channel_id=1, source_target_pairs={{1,0},{2,1},{3,2},{0,3},{5,4},{6,5},{7,6},{4,7},{9,8},{10,9},{11,1... | collective-permute-start | bytes 1179656 | tf_op jit(solution)/shard_map/ppermute | solution.py:12
  17.9 32.0 %collective-permute-start.9 = (s32[1,1,2,4,8]{4,3,2,1,0:T(4,128)S(1)}, s32[1,1,2,4,8]{4,3,2,1,0:T(4,128)S(1)}, u32[]{:S(2)}, u32[]{:S(2)}) collective-permute-start(s32[1,1,2,4,8]{4,3,2,1,0:T(4,128)S(1)} %add_bitcast_fusion), channel_id=1, source_target_pairs={{4,0},{8,4},{12,8},{16,12},{20,16},{24,20},{28,24},{32,28},{36,32}... | collective-permute-start | bytes 776 | tf_op jit(solution)/shard_map/ppermute | solution.py:24
  27.9 8.8 %collective-permute-start.5 = (f32[1,1,4,64,512]{4,3,2,1,0:T(8,128)S(1)}, f32[1,1,4,64,512]{4,3,2,1,0:T(8,128)}, u32[]{:S(2)}, u32[]{:S(2)}) collective-permute-start(f32[1,1,4,64,512]{4,3,2,1,0:T(8,128)S(1)} %get-tuple-element.55), channel_id=1, source_target_pairs={{4,0},{8,4},{12,8},{16,12},{20,16},{24,20},{28,24},{32,28},{36,32}... | collective-permute-start | bytes 1572872 | tf_op jit(solution)/shard_map/ppermute | solution.py:24
  31.2 6.1 %collective-permute-start.4 = (f32[1,1,4,64,512]{4,3,2,1,0:T(8,128)S(1)}, f32[1,1,4,64,512]{4,3,2,1,0:T(8,128)}, u32[]{:S(2)}, u32[]{:S(2)}) collective-permute-start(f32[1,1,4,64,512]{4,3,2,1,0:T(8,128)S(1)} %get-tuple-element.55), channel_id=1, source_target_pairs={{0,4},{4,8},{8,12},{12,16},{16,20},{20,24},{24,28},{28,32},{32,36}... | collective-permute-start | bytes 1572872 | tf_op jit(solution)/shard_map/ppermute | solution.py:21
  31.3 11.3 %collective-permute-start.13 = (f32[1,1,4,64,512]{4,3,2,1,0:T(8,128)S(1)}, f32[1,1,4,64,512]{4,3,2,1,0:T(8,128)S(1)}, u32[]{:S(2)}, u32[]{:S(2)}) collective-permute-start(f32[1,1,4,64,512]{4,3,2,1,0:T(8,128)S(1)} %get-tuple-element.56), channel_id=1, source_target_pairs={{4,0},{8,4},{12,8},{16,12},{20,16},{24,20},{28,24},{32,28},{36,32}... | collective-permute-start | bytes 1572872 | tf_op jit(solution)/shard_map/ppermute | solution.py:24
  34.2 11.4 %collective-permute-start.12 = (f32[1,1,4,64,512]{4,3,2,1,0:T(8,128)S(1)}, f32[1,1,4,64,512]{4,3,2,1,0:T(8,128)S(1)}, u32[]{:S(2)}, u32[]{:S(2)}) collective-permute-start(f32[1,1,4,64,512]{4,3,2,1,0:T(8,128)S(1)} %get-tuple-element.56), channel_id=1, source_target_pairs={{0,4},{4,8},{8,12},{12,16},{16,20},{20,24},{24,28},{28,32},{32,36}... | collective-permute-start | bytes 1572872 | tf_op jit(solution)/shard_map/ppermute | solution.py:21
  39.9 70.1 %collective-permute-start.7 = (f32[3,1,4,64,512]{4,3,2,1,0:T(8,128)}, f32[3,1,4,64,512]{4,3,2,1,0:T(8,128)}, u32[]{:S(2)}, u32[]{:S(2)}) collective-permute-start(f32[3,1,4,64,512]{4,3,2,1,0:T(8,128)} %pad_maximum_fusion.4), channel_id=1, source_target_pairs={{1,0},{2,1},{3,2},{0,3},{5,4},{6,5},{7,6},{4,7},{9,8},{10,9},{11,1... | collective-permute-start | bytes 4718600 | tf_op jit(solution)/shard_map/ppermute | solution.py:24
  42.6 67.4 %collective-permute-start.6 = (f32[3,1,4,64,512]{4,3,2,1,0:T(8,128)}, f32[3,1,4,64,512]{4,3,2,1,0:T(8,128)}, u32[]{:S(2)}, u32[]{:S(2)}) collective-permute-start(f32[3,1,4,64,512]{4,3,2,1,0:T(8,128)} %pad_maximum_fusion.4), channel_id=1, source_target_pairs={{0,1},{1,2},{2,3},{3,0},{4,5},{5,6},{6,7},{7,4},{8,9},{9,10},{10,1... | collective-permute-start | bytes 4718600 | tf_op jit(solution)/shard_map/ppermute | solution.py:21
  42.6 3.0 copy-start.4
  42.6 9.3 %collective-permute-start.8 = (s32[1,1,2,4,8]{4,3,2,1,0:T(4,128)S(1)}, s32[1,1,2,4,8]{4,3,2,1,0:T(4,128)S(1)}, u32[]{:S(2)}, u32[]{:S(2)}) collective-permute-start(s32[1,1,2,4,8]{4,3,2,1,0:T(4,128)S(1)} %add_bitcast_fusion), channel_id=1, source_target_pairs={{0,4},{4,8},{8,12},{12,16},{16,20},{20,24},{24,28},{28,32},{32,36}... | collective-permute-start | bytes 776 | tf_op jit(solution)/shard_map/ppermute | solution.py:21
  45.6 1.4 copy-start.6
  47.0 72.2 %collective-permute-start.15 = (f32[3,1,4,64,512]{4,3,2,1,0:T(8,128)}, f32[3,1,4,64,512]{4,3,2,1,0:T(8,128)}, u32[]{:S(2)}, u32[]{:S(2)}) collective-permute-start(f32[3,1,4,64,512]{4,3,2,1,0:T(8,128)} %pad_maximum_fusion.5), channel_id=1, source_target_pairs={{1,0},{2,1},{3,2},{0,3},{5,4},{6,5},{7,6},{4,7},{9,8},{10,9},{11,1... | collective-permute-start | bytes 4718600 | tf_op jit(solution)/shard_map/ppermute | solution.py:24
  49.9 69.3 %collective-permute-start.14 = (f32[3,1,4,64,512]{4,3,2,1,0:T(8,128)}, f32[3,1,4,64,512]{4,3,2,1,0:T(8,128)}, u32[]{:S(2)}, u32[]{:S(2)}) collective-permute-start(f32[3,1,4,64,512]{4,3,2,1,0:T(8,128)} %pad_maximum_fusion.5), channel_id=1, source_target_pairs={{0,1},{1,2},{2,3},{3,0},{4,5},{5,6},{6,7},{7,4},{8,9},{9,10},{10,1... | collective-permute-start | bytes 4718600 | tf_op jit(solution)/shard_map/ppermute | solution.py:21
  52.0 50.2 %collective-permute-start.11 = (s32[3,1,2,4,8]{4,3,2,1,0:T(4,128)S(1)}, s32[3,1,2,4,8]{4,3,2,1,0:T(4,128)S(1)}, u32[]{:S(2)}, u32[]{:S(2)}) collective-permute-start(s32[3,1,2,4,8]{4,3,2,1,0:T(4,128)S(1)} %pad_add_fusion.1), channel_id=1, source_target_pairs={{1,0},{2,1},{3,2},{0,3},{5,4},{6,5},{7,6},{4,7},{9,8},{10,9},{11,1... | collective-permute-start | bytes 2312 | tf_op jit(solution)/shard_map/ppermute | solution.py:24
  102.1 5.2 collective-permute-start.10
  114.0 5.2 copy-start.5
  114.0 5.2 copy-start.7
  143.9 7.1 %copy-start.3 = (f32[4,64,8,64]{3,2,1,0:T(8,128)S(1)}, f32[4,64,8,64]{3,2,1,0:T(8,128)}, u32[]{:S(2)}) copy-start(f32[4,64,8,64]{3,2,1,0:T(8,128)} %reshape_squeeze.3) | copy-start | bytes 1572868
  151.0 20.7 %copy-start = (f32[4,8,64,8,64]{4,3,2,1,0:T(8,128)S(1)}, f32[4,8,64,8,64]{4,3,2,1,0:T(8,128)}, u32[]{:S(2)}) copy-start(f32[4,8,64,8,64]{4,3,2,1,0:T(8,128)} %reshape.365) | copy-start | bytes 12582916
  164.1 24.6 %slice-start = ((s8[8388608]{0:T(1024)(128)(4,1)}), s8[4194304]{0:T(1024)(128)(4,1)S(1)}, s32[]{:S(2)}) async-start(s8[8388608]{0:T(1024)(128)(4,1)} %bitcast.217), calls=%async_computation | async-start | bytes 8388608
  171.7 17.0 %slice-start.1 = ((s8[8388608]{0:T(1024)(128)(4,1)}), s8[4194304]{0:T(1024)(128)(4,1)S(1)}, s32[]{:S(2)}) async-start(s8[8388608]{0:T(1024)(128)(4,1)} %bitcast.217), calls=%async_computation.1 | async-start | bytes 8388608
  188.7 8.9 %copy-start.1 = (f32[4,64,64,8,1]{2,3,4,1,0:T(8,128)}, f32[4,64,64,8,1]{2,3,4,1,0:T(8,128)S(1)}, u32[]{:S(2)}) copy-start(f32[4,64,64,8,1]{2,3,4,1,0:T(8,128)S(1)} %fusion.12) | copy-start | bytes 1572868
  205.6 9.1 %copy-start.2 = (f32[4,64,64,8,1]{2,3,4,1,0:T(8,128)S(1)}, f32[4,64,64,8,1]{2,3,4,1,0:T(8,128)}, u32[]{:S(2)}) copy-start(f32[4,64,64,8,1]{2,3,4,1,0:T(8,128)} %copy-done.1) | copy-start | bytes 1572868
  314.2 6.7 %collective-permute-start.16 = (f32[1,1,4,64,512]{4,3,2,1,0:T(8,128)S(1)}, f32[1,1,4,64,512]{4,3,2,1,0:T(8,128)S(1)}, u32[]{:S(2)}, u32[]{:S(2)}) collective-permute-start(f32[1,1,4,64,512]{4,3,2,1,0:T(8,128)S(1)} %mul.132), channel_id=1, source_target_pairs={{0,4},{4,8},{8,12},{12,16},{16,20},{20,24},{24,28},{28,32},{32,36}... | collective-permute-start | bytes 1572872 | tf_op jit(solution)/shard_map/ppermute | solution.py:21
  314.8 8.9 %collective-permute-start.17 = (f32[1,1,4,64,512]{4,3,2,1,0:T(8,128)S(1)}, f32[1,1,4,64,512]{4,3,2,1,0:T(8,128)S(1)}, u32[]{:S(2)}, u32[]{:S(2)}) collective-permute-start(f32[1,1,4,64,512]{4,3,2,1,0:T(8,128)S(1)} %mul.132), channel_id=1, source_target_pairs={{4,0},{8,4},{12,8},{16,12},{20,16},{24,20},{28,24},{32,28},{36,32}... | collective-permute-start | bytes 1572872 | tf_op jit(solution)/shard_map/ppermute | solution.py:24
  323.8 32.9 %collective-permute-start.19 = (f32[3,1,4,64,512]{4,3,2,1,0:T(8,128)S(1)}, f32[3,1,4,64,512]{4,3,2,1,0:T(8,128)S(1)}, u32[]{:S(2)}, u32[]{:S(2)}) collective-permute-start(f32[3,1,4,64,512]{4,3,2,1,0:T(8,128)S(1)} %constant_dynamic-update-slice_fusion), channel_id=1, source_target_pairs={{1,0},{2,1},{3,2},{0,3},{5,4},{6,5},{7,6},{4,7},{9,8},{10,9},{11,1... | collective-permute-start | bytes 4718600 | tf_op jit(solution)/shard_map/ppermute | solution.py:24
  325.6 33.8 %collective-permute-start.18 = (f32[3,1,4,64,512]{4,3,2,1,0:T(8,128)S(1)}, f32[3,1,4,64,512]{4,3,2,1,0:T(8,128)S(1)}, u32[]{:S(2)}, u32[]{:S(2)}) collective-permute-start(f32[3,1,4,64,512]{4,3,2,1,0:T(8,128)S(1)} %constant_dynamic-update-slice_fusion), channel_id=1, source_target_pairs={{0,1},{1,2},{2,3},{3,0},{4,5},{5,6},{6,7},{7,4},{8,9},{9,10},{10,1... | collective-permute-start | bytes 4718600 | tf_op jit(solution)/shard_map/ppermute | solution.py:21
  392.1 28.5 %slice-start.2 = ((s8[8388608]{0:T(1024)(128)(4,1)}), s8[4194304]{0:T(1024)(128)(4,1)S(1)}, s32[]{:S(2)}) async-start(s8[8388608]{0:T(1024)(128)(4,1)} %bitcast.219), calls=%async_computation.2 | async-start | bytes 8388608
  399.7 20.9 %slice-start.3 = ((s8[8388608]{0:T(1024)(128)(4,1)}), s8[4194304]{0:T(1024)(128)(4,1)S(1)}, s32[]{:S(2)}) async-start(s8[8388608]{0:T(1024)(128)(4,1)} %bitcast.219), calls=%async_computation.3 | async-start | bytes 8388608
where the time goes:
time: 603 us; the launch traced here: 593 us
  blocking collectives  237 us (39%)
  matrix products  150 us (25%)
  waiting for transfers between devices  78.6 us (13%)
  local copies, waits for them, and re-layouts  45.3 us (8%)
  other arithmetic  36.2 us (6%)
  starting transfers between devices  33.4 us (6%)
  between operations  13.4 us (2%)
    dot_general x8, matrix products, local_product(): jnp.einsum('ipar,iarcq->iapcq', left_rows.reshape(groups, width, kept, wi...  88.9 us
    psum x1, blocking collectives, global_count(): return lax.psum(value, ('gx', 'gy'))  86.8 us
    psum x1, blocking collectives, shards(): scale_last = count_start / lax.psum(jnp.sum(mixed * ovl_rows), ('gx', 'gy'))  75.5 us
    psum x1, blocking collectives, shards(): lax.psum(jnp.sum(den_rows * ham_rows), ('gx', 'gy'))  74.3 us
    ppermute x8, waiting for transfers between devices, with_halo(): lax.ppermute(lax.slice_in_dim(block, 0, width, axis=dim), axis, backward)  62.5 us
    dot_general x8, matrix products, local_product(): jnp.einsum('iabc,iapcq->ipbq', matches, partial_rows, precision=lax.Preci...  61.1 us
    ppermute x8, starting transfers between devices, with_halo(): lax.ppermute(lax.slice_in_dim(block, 0, width, axis=dim), axis, backward)  23 us
    reshape x3, local copies, waits for them, and re-layouts, local_product(): gathered = gathered.reshape(groups, kept, width, kept, width)  21.2 us
  transfers between devices with their start and end apart: 20, of which 9 were waited for; matrix products, arithmetic and copies ran while one was open for 7% of the time, Pallas kernels for 0%

commit v1 on v0

v1 whole, which is shorter than its diff:
```python
import functools

import jax
import jax.numpy as jnp
from jax import lax
from jax.experimental import pallas as pl
from jax.experimental.pallas import tpu as pltpu
from jax.sharding import PartitionSpec as P

MESH = pl.DeviceIdType.MESH
F32, BF16, I32 = jnp.float32, jnp.bfloat16, jnp.int32
A, B, C, D = range(4)
SIDE, KEPT, TYPES = 64, 8, 4
COLUMNS = SIDE * KEPT
OVL, DEN, MIX = range(3)
BEHIND = (1, 0, 3, 2)
AROUND = [(ux, uy) for ux in (-1, 0, 1) for uy in (-1, 0, 1) if (ux, uy) != (0, 0)]
LOW = 4


def row_id(dx, dy, kind):
    return (3 * (dx + 1) + (dy + 1)) * TYPES + kind


def domain_key(code):
    across = (code * 11) >> 5
    return (across - 1) * 64 + (code - 3 * across - 1) * 8


def folded(tile):
    return jnp.sum(tile.reshape(tile.shape[0] // 8, 8, 128), axis=0)


def kernel(
    nx, ny,
    ham, ovl, den, leaving, codes, slots,
    out, energy,
    rim, ham_out, ham_home, tiles_s, tiles_p, lhs, second, last,
    near, near_s, index_v, index_s, near_sums, far_sums,
    send_sem, recv_sem, ham_send, ham_recv, near_send, near_recv, sum_send, sum_recv, local_sem,
):
    x, y = lax.axis_index("gx"), lax.axis_index("gy")
    high = nx // LOW
    group = LOW * ny
    at_high, at_low = x // LOW, (x % LOW) * ny + y

    def beside(ux, uy):
        return (lax.rem(x + ux + nx, nx), lax.rem(y + uy + ny, ny))

    def near_peer(j):
        return (at_high * LOW + j // ny, j % ny)

    def far_peer(j):
        return (j * LOW + x % LOW, y)

    barrier = pltpu.get_barrier_semaphore()
    for ux, uy in AROUND:
        pl.semaphore_signal(barrier, inc=1, device_id=beside(ux, uy), device_id_type=MESH)

    def greet_near(o, carry):
        pl.semaphore_signal(barrier, inc=1, device_id=near_peer((at_low + o) % group), device_id_type=MESH)
        return carry

    def greet_far(o, carry):
        pl.semaphore_signal(barrier, inc=1, device_id=far_peer((at_high + o) % high), device_id_type=MESH)
        return carry

    lax.fori_loop(1, group, greet_near, 0)
    lax.fori_loop(1, high, greet_far, 0)

    lane = lax.broadcasted_iota(I32, (8, 128), 1)
    sub = lax.broadcasted_iota(I32, (8, 128), 0)

    start = jnp.zeros((8, 128), F32)
    for kind in range(TYPES):
        slot = leaving[kind]
        mine = row_id(*((1, 0), (-1, 0), (0, 1), (0, -1))[kind], kind)
        s_row, p_row = ovl[0, 0, slot], den[0, 0, slot]
        rim[OVL, mine] = s_row
        rim[DEN, mine] = p_row
        prod = s_row * p_row
        for k in range(COLUMNS // 128):
            start += folded(prod[:, k * 128 : (k + 1) * 128])

    note = jnp.zeros((8, 128), I32)
    for kind in range(TYPES):
        slot = leaving[BEHIND[kind]]
        for c in range(KEPT):
            key = domain_key(codes[slot, c]) + slots[slot, c]
            note = jnp.where((sub == kind) & (lane == c), key, note)
        note = jnp.where((sub == TYPES) & (lane == slot), kind, note)
    near[4] = note

    pl.semaphore_wait(barrier, len(AROUND) + group - 1 + high - 1)

    def row_copy(m, dx, dy, kind, ux, uy):
        there = row_id(dx - ux, dy - uy, kind)
        return pltpu.make_async_remote_copy(
            src_ref=rim.at[m, row_id(dx, dy, kind)],
            dst_ref=rim.at[m, there],
            send_sem=send_sem.at[m, there],
            recv_sem=recv_sem.at[m, there],
            device_id=beside(ux, uy),
            device_id_type=MESH,
        )

    flying = {}

    def send(m, dx, dy, kind, ux, uy):
        copy = row_copy(m, dx, dy, kind, ux, uy)
        copy.start()
        flying[m, dx - ux, dy - uy, kind] = copy

    def initial(m):
        send(m, 0, 1, C, 0, 1)
        send(m, 0, -1, D, 0, -1)
        send(m, 1, 0, A, 1, 0)
        send(m, -1, 0, B, -1, 0)
        for u in (1, -1):
            send(m, 1, 0, A, 0, u)
            send(m, -1, 0, B, 0, u)
        for u in (1, -1):
            send(m, 0, 1, C, u, 0)
            send(m, 0, -1, D, u, 0)

    near_copies = []

    def tell_pattern():
        for k, (ux, uy) in enumerate(AROUND):
            there = row_id(-ux, -uy, 0) // TYPES
            copy = pltpu.make_async_remote_copy(
                src_ref=near.at[4],
                dst_ref=near.at[there],
                send_sem=near_send.at[there],
                recv_sem=near_recv.at[there],
                device_id=beside(ux, uy),
                device_id_type=MESH,
            )
            copy.start()
            near_copies.append(copy)

    tell_pattern()
    initial(OVL)
    initial(DEN)

    def arrive(m, dx, dy, kind):
        flying[m, dx, dy, kind].wait_recv()

    def first_tier(m):
        arrive(m, 0, 0, C)
        send(m, 0, 0, C, 0, 1)
        for u in (1, -1):
            send(m, 0, 0, C, u, 0)
        arrive(m, 0, 0, D)
        send(m, 0, 0, D, 0, -1)
        for u in (1, -1):
            send(m, 0, 0, D, u, 0)
        arrive(m, 0, 0, A)
        send(m, 0, 0, A, 1, 0)
        arrive(m, 0, 0, B)
        send(m, 0, 0, B, -1, 0)
        for u in (1, -1):
            arrive(m, 1, u, A)
            send(m, 1, u, A, 1, 0)
            arrive(m, -1, u, B)
            send(m, -1, u, B, -1, 0)

    def second_tier(m):
        arrive(m, 0, -1, C)
        for u in (1, -1):
            send(m, 0, -1, C, u, 0)
        arrive(m, 0, 1, D)
        for u in (1, -1):
            send(m, 0, 1, D, u, 0)
        for u in (1, -1):
            arrive(m, 0, u, A)
            send(m, 0, u, A, 1, 0)
            arrive(m, 0, u, B)
            send(m, 0, u, B, -1, 0)

    half = lax.broadcasted_iota(I32, (16, 128), 1) < SIDE

    def split_row(m, which, tiles, scale=None):
        def strip(k, carry):
            rows = pl.ds(pl.multiple_of(k * 16, 16), 16)
            for pair in range(KEPT // 2):
                v = rim[m, which, rows, pair * 128 : (pair + 1) * 128]
                if scale is not None:
                    v = v * scale
                top = v.astype(BF16).astype(F32)
                rest = pltpu.roll(v - top, SIDE, 1)
                tiles[(which + 1) * KEPT + 2 * pair, rows, :] = jnp.where(half, top, rest).astype(BF16)
                tiles[(which + 1) * KEPT + 2 * pair + 1, rows, :] = jnp.where(half, rest, top).astype(BF16)
            return carry

        lax.fori_loop(0, SIDE // 16, strip, 0)

    def split_left(into, i, columns, v):
        top = v.astype(BF16)
        lhs[into, i, 0:SIDE, columns] = top
        lhs[into, i, SIDE : 2 * SIDE, columns] = (v - top.astype(F32)).astype(BF16)

    def left_rows(m, scale=None):
        for i in range(TYPES):
            v = rim[m, row_id(0, 0, i)]
            split_left(0, i, slice(None), v if scale is None else v * scale)

    wide = lax.broadcasted_iota(I32, (SIDE, 128), 1) < SIDE

    def product(left, tiles, emit, after=None, carry=0):
        def one_row(i, carry):
            a = lhs[left, i]
            for pair in range(KEPT // 2):
                right = jnp.concatenate(
                    [
                        jnp.concatenate([tiles[index_s[i * KEPT + b, e]] for e in range(KEPT)], axis=0)
                        for b in (2 * pair, 2 * pair + 1)
                    ],
                    axis=1,
                )
                full = jnp.dot(a, right, preferred_element_type=F32)
                both = full[:SIDE] + full[SIDE:]
                even, odd = both[:, :128], both[:, 128:]
                even = even + pltpu.roll(even, SIDE, 1)
                odd = odd + pltpu.roll(odd, SIDE, 1)
                carry = emit(i, slice(pair * 128, (pair + 1) * 128), jnp.where(wide, even, odd), carry)
            if after is not None:
                after(i)
            return carry

        return lax.fori_loop(0, TYPES, one_row, carry)

    def to_left(into):
        def emit(i, columns, v, carry):
            split_left(into, i, columns, v)
            return carry

        return emit

    def to_left_and_second(into):
        def emit(i, columns, v, carry):
            split_left(into, i, columns, v)
            second[i, :, columns] = v
            return carry

        return emit

    own = row_id(0, 0, 0)

    for k in range(KEPT):
        tiles_s[k] = jnp.zeros((SIDE, 128), BF16)
        tiles_p[k] = jnp.zeros((SIDE, 128), BF16)
    for copy in near_copies:
        copy.wait_recv()
    to_scalars = pltpu.make_async_copy(near, near_s, local_sem.at[0])
    to_scalars.start()
    to_scalars.wait()

    first_tier(OVL)

    for kind in range(TYPES):
        slot = leaving[BEHIND[kind]]
        mine = jnp.zeros((8, 128), I32)
        for b in range(KEPT):
            mine = jnp.where(sub == b, domain_key(codes[slot, b]) + slots[slot, b], mine)
        found = jnp.zeros((8, 128), I32)
        for a in range(KEPT):
            code = codes[slot, a]
            what = near_s[code, TYPES, slots[slot, a]]
            keys = near[code, pl.ds(what, 1), :] + domain_key(code)
            hit = (keys == mine) & (lane < KEPT)
            tile = jnp.where(hit, (code * TYPES + what + 1) * KEPT + lane, 0)
            found = jnp.where(lane == a, jnp.sum(tile, axis=1, keepdims=True), found)
        index_v[kind * KEPT : (kind + 1) * KEPT, :] = found
    to_scalars = pltpu.make_async_copy(index_v, index_s, local_sem.at[1])
    to_scalars.start()
    to_scalars.wait()

    second_tier(OVL)
    first_tier(DEN)
    left_rows(DEN)

    def middle(m, tiles, scale=None):
        for dy in (0, 1, -1):
            for kind in range(TYPES):
                split_row(m, row_id(0, dy, kind), tiles, scale)
        for dy in (0, 1, -1):
            split_row(m, row_id(1, dy, A), tiles, scale)
            split_row(m, row_id(-1, dy, B), tiles, scale)

    def third_tier(m, tiles):
        for dy in (0, 1, -1):
            for u, kinds in ((1, (B, C, D)), (-1, (A, C, D))):
                for kind in kinds:
                    arrive(m, u, dy, kind)
                    split_row(m, row_id(u, dy, kind), tiles)

    middle(OVL, tiles_s)
    third_tier(OVL, tiles_s)
    second_tier(DEN)

    ham_copies = []
    for kind in range(TYPES):
        ham_out[kind] = ham[0, 0, leaving[kind]]
    for kind, (ux, uy) in enumerate(((1, 0), (-1, 0), (0, 1), (0, -1))):
        copy = pltpu.make_async_remote_copy(
            src_ref=ham_out.at[kind],
            dst_ref=ham_home.at[kind],
            send_sem=ham_send.at[kind],
            recv_sem=ham_recv.at[kind],
            device_id=beside(ux, uy),
            device_id_type=MESH,
        )
        copy.start()
        ham_copies.append(copy)

    product(0, tiles_s, to_left(1))
    middle(DEN, tiles_p)
    third_tier(DEN, tiles_p)
    product(1, tiles_p, to_left_and_second(0))
    product(0, tiles_s, to_left(1))

    def mixed_out(i, columns, v, total):
        m = 3.0 * second[i, :, columns] - 2.0 * v
        rim[MIX, own + i, :, columns] = m
        return total + folded(m * rim[OVL, own + i, :, columns])

    def mixed_sent(i):
        for ux, uy in ((0, 1), (0, -1), (1, 0), (-1, 0)):
            row_copy(MIX, 0, 0, i, ux, uy).start()

    count = product(1, tiles_p, mixed_out, mixed_sent, jnp.zeros((8, 128), F32))

    def near_copy(s, j, mine):
        return pltpu.make_async_remote_copy(
            src_ref=near_sums.at[s, at_low],
            dst_ref=near_sums.at[s, mine],
            send_sem=sum_send.at[s, 0, j],
            recv_sem=sum_recv.at[s, 0, mine],
            device_id=near_peer(j),
            device_id_type=MESH,
        )

    def far_copy(s, j, mine):
        return pltpu.make_async_remote_copy(
            src_ref=far_sums.at[s, at_high],
            dst_ref=far_sums.at[s, mine],
            send_sem=sum_send.at[s, 1, j],
            recv_sem=sum_recv.at[s, 1, mine],
            device_id=far_peer(j),
            device_id_type=MESH,
        )

    def spread(copy_of, s, me, members):
        def step(o, carry):
            copy_of(s, (me + o) % members, me).start()
            return carry

        lax.fori_loop(1, members, step, 0)

    def collect(copy_of, s, me, members):
        def step(o, carry):
            j = (me + o) % members
            copy_of(s, j, j).wait_recv()
            return carry

        lax.fori_loop(1, members, step, 0)

    def sent(copy_of, s, me, members):
        def step(o, carry):
            copy_of(s, (me + o) % members, me).wait_send()
            return carry

        lax.fori_loop(1, members, step, 0)

    near_sums[0, at_low, 0] = start
    near_sums[0, at_low, 1] = count
    near_sums[0, at_low, 2] = count
    spread(near_copy, 0, at_low, group)


    def pass_on(i):
        for dy in (-1, 1):
            row_copy(MIX, 0, 0, i, 0, -dy).wait_recv()
            for u in (1, -1):
                row_copy(MIX, 0, dy, i, u, 0).start()

    pass_on(0)
    collect(near_copy, 0, at_low, group)
    far_sums[0, at_high, 0] = jnp.sum(near_sums[0, :, 0], axis=0)
    far_sums[0, at_high, 1] = jnp.sum(near_sums[0, :, 1], axis=0)
    far_sums[0, at_high, 2] = count
    spread(far_copy, 0, at_high, high)
    pass_on(1)
    pass_on(2)
    pass_on(3)
    collect(far_copy, 0, at_high, high)

    def over_all(tile):
        return jnp.sum(jnp.sum(tile, axis=1, keepdims=True), axis=0, keepdims=True)

    count_start = over_all(jnp.sum(far_sums[0, :, 0], axis=0))
    scale = count_start / over_all(jnp.sum(far_sums[0, :, 1], axis=0))
    left_rows(MIX, scale)
    product(0, tiles_s, to_left(1))
    for dy in (0, -1, 1):
        for kind in range(TYPES):
            split_row(MIX, row_id(0, dy, kind), tiles_p, scale)
    for dy in (0, -1, 1):
        for u in (1, -1):
            for kind in range(TYPES):
                row_copy(MIX, 0, dy, kind, -u, 0).wait_recv()
                split_row(MIX, row_id(u, dy, kind), tiles_p, scale)
    product(1, tiles_p, to_left_and_second(0))
    product(0, tiles_s, to_left(1))

    def last_out(i, columns, v, carry):
        total, largest = carry
        m = 3.0 * second[i, :, columns] - 2.0 * v
        last[i, :, columns] = m
        return (
            total + folded(m * rim[OVL, own + i, :, columns]),
            jnp.maximum(largest, jnp.max(jnp.abs(m).reshape(SIDE // 8, 8, 128), axis=0)),
        )

    zero = jnp.zeros((8, 128), F32)
    count, largest = product(1, tiles_p, last_out, None, (zero, zero))
    for copy in ham_copies:
        copy.wait_recv()
    largest = jnp.max(jnp.max(largest, axis=1, keepdims=True), axis=0, keepdims=True)
    size = jnp.where(largest > 1e-37, jnp.minimum(largest, 1e37), 1.0)
    inverse = 1.0 / size
    band = zero
    for i in range(TYPES):
        for k in range(COLUMNS // 128):
            columns = slice(k * 128, (k + 1) * 128)
            band += folded((last[i, :, columns] * inverse) * ham_home[i, :, columns])

    def joined(sums):
        sizes = sums[:, 2]
        biggest = jnp.max(sizes, axis=0)
        return jnp.sum(sums[:, 0], axis=0), jnp.sum(sums[:, 1] * (sizes / biggest[None]), axis=0), biggest

    near_sums[1, at_low, 0] = count
    near_sums[1, at_low, 1] = band
    near_sums[1, at_low, 2] = jnp.broadcast_to(size, (8, 128))
    spread(near_copy, 1, at_low, group)
    collect(near_copy, 1, at_low, group)
    part = joined(near_sums[1])
    for k in range(3):
        far_sums[1, at_high, k] = part[k]
    spread(far_copy, 1, at_high, high)
    collect(far_copy, 1, at_high, high)
    count, band, size = joined(far_sums[1])
    scale = count_start / over_all(count)
    for slot in range(TYPES):
        out[0, 0, slot] = scale * last[near_s[4, TYPES, slot]]
    basis = nx * ny * TYPES * SIDE
    energy[0] = jnp.sum(over_all(band * (size * scale))) / basis

    for copy in (*near_copies, *ham_copies, *flying.values()):
        copy.wait_send()
    for i in range(TYPES):
        for ux, uy in ((0, 1), (0, -1), (1, 0), (-1, 0)):
            row_copy(MIX, 0, 0, i, ux, uy).wait_send()
        for dy in (-1, 1):
            for u in (1, -1):
                row_copy(MIX, 0, dy, i, u, 0).wait_send()
    for s in range(2):
        sent(near_copy, s, at_low, group)
        sent(far_copy, s, at_high, high)


def shards(nx, ny, ham, ovl, den, leaving, codes, slots):
    high, group = nx // LOW, LOW * ny
    vmem = pl.BlockSpec(memory_space=pltpu.VMEM)
    smem = pl.BlockSpec(memory_space=pltpu.SMEM)
    dma = pltpu.SemaphoreType.DMA
    purified, energy = pl.pallas_call(
        functools.partial(kernel, nx, ny),
        out_shape=(
            jax.ShapeDtypeStruct(den.shape, F32),
            jax.ShapeDtypeStruct((1,), F32),
        ),
        in_specs=[vmem] * 3 + [smem] * 3,
        out_specs=(vmem, smem),
        scratch_shapes=[
            pltpu.VMEM((3, 9 * TYPES, SIDE, COLUMNS), F32),
            pltpu.VMEM((TYPES, SIDE, COLUMNS), F32),
            pltpu.VMEM((TYPES, SIDE, COLUMNS), F32),
            pltpu.VMEM(((9 * TYPES + 1) * KEPT, SIDE, 128), BF16),
            pltpu.VMEM(((9 * TYPES + 1) * KEPT, SIDE, 128), BF16),
            pltpu.VMEM((2, TYPES, 2 * SIDE, COLUMNS), BF16),
            pltpu.VMEM((TYPES, SIDE, COLUMNS), F32),
            pltpu.VMEM((TYPES, SIDE, COLUMNS), F32),
            pltpu.VMEM((9, 8, 128), I32),
            pltpu.SMEM((9, 8, 128), I32),
            pltpu.VMEM((TYPES * KEPT, 128), I32),
            pltpu.SMEM((TYPES * KEPT, 128), I32),
            pltpu.VMEM((2, group, 3, 8, 128), F32),
            pltpu.VMEM((2, high, 3, 8, 128), F32),
            dma((3, 9 * TYPES)),
            dma((3, 9 * TYPES)),
            dma((TYPES,)),
            dma((TYPES,)),
            dma((9,)),
            dma((9,)),
            dma((2, 2, max(group, high))),
            dma((2, 2, max(group, high))),
            dma((2,)),
        ],
        compiler_params=pltpu.CompilerParams(
            collective_id=0, has_side_effects=True, vmem_limit_bytes=48 * 1024 * 1024
        ),
    )(
        ham, ovl, den,
        leaving.reshape(TYPES), codes.reshape(TYPES, KEPT), slots.reshape(TYPES, KEPT),
    )
    return purified, energy.reshape(())


def solution(mesh):
    whole = P("gx", "gy", None, None, None)
    few = P("gx", "gy", None, None)
    return jax.shard_map(
        functools.partial(shards, mesh.shape["gx"], mesh.shape["gy"]),
        mesh=mesh,
        in_specs=(whole, whole, whole, few, few, few),
        out_specs=(whole, P()),
        check_vma=False,
    )
```

time: 603 us -> 135 us (0.22); the launches traced: 593 us -> 135 us
  blocking collectives: 237 us -> 0 us
  matrix products: 150 us -> 0 us
  Pallas kernels: 0 us -> 128 us
  waiting for transfers between devices: 78.6 us -> 0 us
  local copies, waits for them, and re-layouts: 45.3 us -> 4.6 us
  other arithmetic: 36.2 us -> 0 us
  starting transfers between devices: 33.4 us -> 0 us
  between operations: 13.4 us -> 2.49 us
    psum x3 -> x0, blocking collectives: 237 us -> none  [the longest x1 86.8 us: global_count(): return lax.psum(value, ('gx', 'gy'))]
    dot_general x16 -> x0, matrix products: 150 us -> none  [the longest x8 88.9 us: local_product(): jnp.einsum('ipar,iarcq->iapcq', left_rows.reshape(groups, width, kept, wi...]
    pallas_call x0 -> x1, Pallas kernels: none -> 128 us  [shards(): pl.pallas_call(functools.partial(kernel, nx, ny), out_shape=(jax.ShapeDty...]
    ppermute x20 -> x0, waiting for transfers between devices: 78.6 us -> none  [the longest x8 62.5 us: with_halo(): lax.ppermute(lax.slice_in_dim(block, 0, width, axis=dim), axis, backward)]
    ppermute x20 -> x0, starting transfers between devices: 33.4 us -> none  [the longest x8 23 us: with_halo(): lax.ppermute(lax.slice_in_dim(block, 0, width, axis=dim), axis, backward)]
    reshape x3 -> x0, local copies, waits for them, and re-layouts: 21.2 us -> none  [local_product(): gathered = gathered.reshape(groups, kept, width, kept, width)]
    gather x5 -> x0, local copies, waits for them, and re-layouts: 16.5 us -> none  [the longest x3 15.4 us: local_product(): jnp.take(rim_rows.reshape(9 * groups, width, columns), row_index.reshape(...]
    select_n x4 -> x0, other arithmetic: 16.3 us -> none  [the longest x3 13.6 us: local_product(): jnp.take(rim_rows.reshape(9 * groups, width, columns), row_index.reshape(...]
  transfers between devices with their start and end apart: 20 -> 0, of which waited for: 9 -> 0; matrix products, arithmetic and copies ran while one was open for 7% -> 0% of each run, Pallas kernels for 0% -> 0%
where the time goes in v1:
time: 135 us
  Pallas kernels  128 us (95%)
  local copies, waits for them, and re-layouts  4.6 us (3%)
  between operations  2.49 us (2%)
    pallas_call x1, Pallas kernels, shards(): pl.pallas_call(functools.partial(kernel, nx, ny), out_shape=(jax.ShapeDty...  128 us
    unnamed x13, local copies, waits for them, and re-layouts  4.6 us

profile of v1, /device:TPU:1, one launch (start us, length us, event | category | flops | bytes accessed | tf_op | source)
XLA Modules:
  0.0 134.9 jit_solution(15696302881835512137)
XLA Ops:
  0.6 0.0 copy-start.4
  0.6 0.0 copy-start.3
  0.7 0.0 copy-start.5
  0.7 0.7 copy-done.4
  1.3 0.0 copy-done.3
  1.3 0.0 copy-done.5
  1.3 0.0 copy-start
  1.3 1.0 copy-done
  2.4 0.0 copy-start.1
  2.4 1.0 copy-done.1
  3.4 0.0 copy-start.2
  3.4 1.0 copy-done.2
  4.5 127.8 %shard_map.77 = (f32[1,1,4,64,512]{4,3,2,1,0:T(8,128)S(1)}, f32[1]{0:T(128)}) custom-call(f32[1,1,4,64,512]{4,3,2,1,0:T(8,128)S(1)} %copy-done, f32[1,1,4,64,512]{4,3,2,1,0:T(8,128)S(1)} %copy-done.1, f32[1,1,4,64,512]{4,3,2,1,0:T(8,128)S(1)} %copy-done.2, s32[4]{0:T(128)S(1)} %bitcast.6, s32[4,8]{1,0:T(4,128)S(1)} %bitcast.4, s32[4,8]{1,0:T(4,128)S(1)} %bitcast.5), custom_call_target="tpu_custom_call" | custom-call | tf_op jit(solution)/shard_map/pallas_call | solution.py:479
  132.3 0.8 copy.10
Async XLA Ops:
  0.6 0.7 copy-start.4
  0.6 0.7 copy-start.3
  0.7 0.7 copy-start.5
  1.3 1.0 copy-start
  2.4 1.0 copy-start.1
  3.4 1.0 copy-start.2

commit v2 on v1

--- a/solution.py
+++ b/solution.py
@@ -178,22 +178,17 @@
             arrive(m, 0, u, B)
             send(m, 0, u, B, -1, 0)
 
-    half = lax.broadcasted_iota(I32, (16, 128), 1) < SIDE
+    half = lax.broadcasted_iota(I32, (SIDE, 128), 1) < SIDE
 
     def split_row(m, which, tiles, scale=None):
-        def strip(k, carry):
-            rows = pl.ds(pl.multiple_of(k * 16, 16), 16)
-            for pair in range(KEPT // 2):
-                v = rim[m, which, rows, pair * 128 : (pair + 1) * 128]
-                if scale is not None:
-                    v = v * scale
-                top = v.astype(BF16).astype(F32)
-                rest = pltpu.roll(v - top, SIDE, 1)
-                tiles[(which + 1) * KEPT + 2 * pair, rows, :] = jnp.where(half, top, rest).astype(BF16)
-                tiles[(which + 1) * KEPT + 2 * pair + 1, rows, :] = jnp.where(half, rest, top).astype(BF16)
-            return carry
-
-        lax.fori_loop(0, SIDE // 16, strip, 0)
+        for pair in range(KEPT // 2):
+            v = rim[m, which, :, pair * 128 : (pair + 1) * 128]
+            if scale is not None:
+                v = v * scale
+            top = v.astype(BF16)
+            rest = pltpu.roll((v - top.astype(F32)).astype(BF16), SIDE, 1)
+            tiles[(which + 1) * KEPT + 2 * pair] = jnp.where(half, top, rest)
+            tiles[(which + 1) * KEPT + 2 * pair + 1] = jnp.where(half, rest, top)
 
     def split_left(into, i, columns, v):
         top = v.astype(BF16)
@@ -280,20 +275,40 @@
     first_tier(DEN)
     left_rows(DEN)
 
-    def middle(m, tiles, scale=None):
-        for dy in (0, 1, -1):
-            for kind in range(TYPES):
-                split_row(m, row_id(0, dy, kind), tiles, scale)
-        for dy in (0, 1, -1):
-            split_row(m, row_id(1, dy, A), tiles, scale)
-            split_row(m, row_id(-1, dy, B), tiles, scale)
+    def landed(m, which):
+        pltpu.make_async_remote_copy(
+            src_ref=rim.at[m, which],
+            dst_ref=rim.at[m, which],
+            send_sem=send_sem.at[m, which],
+            recv_sem=recv_sem.at[m, which],
+            device_id=beside(1, 0),
+            device_id_type=MESH,
+        ).wait_recv()
+
+    def middle(m, tiles):
+        def one(j, carry):
+            split_row(m, row_id(0, -1, 0) + j, tiles)
+            return carry
+
+        def sides(j, carry):
+            split_row(m, row_id(1, -1, A) + j * TYPES, tiles)
+            split_row(m, row_id(-1, -1, B) + j * TYPES, tiles)
+            return carry
+
+        lax.fori_loop(0, 3 * TYPES, one, 0)
+        lax.fori_loop(0, 3, sides, 0)
 
     def third_tier(m, tiles):
-        for dy in (0, 1, -1):
+        def one(j, carry):
+            skip = lax.rem(j + 1, 3) * TYPES
             for u, kinds in ((1, (B, C, D)), (-1, (A, C, D))):
                 for kind in kinds:
-                    arrive(m, u, dy, kind)
-                    split_row(m, row_id(u, dy, kind), tiles)
+                    which = row_id(u, -1, kind) + skip
+                    landed(m, which)
+                    split_row(m, which, tiles)
+            return carry
+
+        lax.fori_loop(0, 3, one, 0)
 
     middle(OVL, tiles_s)
     third_tier(OVL, tiles_s)
@@ -373,9 +388,12 @@
 
         lax.fori_loop(1, members, step, 0)
 
-    near_sums[0, at_low, 0] = start
-    near_sums[0, at_low, 1] = count
-    near_sums[0, at_low, 2] = count
+    across = lax.broadcasted_iota(I32, (1, 128), 1)
+
+    def over_all(tile):
+        return jnp.sum(jnp.sum(tile, axis=0, keepdims=True), axis=1, keepdims=True)
+
+    near_sums[0, at_low] = jnp.where(across < SIDE, over_all(start), over_all(count))
     spread(near_copy, 0, at_low, group)
 
 
@@ -387,30 +405,34 @@
 
     pass_on(0)
     collect(near_copy, 0, at_low, group)
-    far_sums[0, at_high, 0] = jnp.sum(near_sums[0, :, 0], axis=0)
-    far_sums[0, at_high, 1] = jnp.sum(near_sums[0, :, 1], axis=0)
-    far_sums[0, at_high, 2] = count
+    far_sums[0, at_high] = jnp.sum(near_sums[0], axis=0)
     spread(far_copy, 0, at_high, high)
     pass_on(1)
     pass_on(2)
     pass_on(3)
     collect(far_copy, 0, at_high, high)
 
-    def over_all(tile):
-        return jnp.sum(jnp.sum(tile, axis=1, keepdims=True), axis=0, keepdims=True)
-
-    count_start = over_all(jnp.sum(far_sums[0, :, 0], axis=0))
-    scale = count_start / over_all(jnp.sum(far_sums[0, :, 1], axis=0))
+    counts = jnp.sum(far_sums[0], axis=0)
+    count_start = counts[:, :1]
+    scale = count_start / counts[:, SIDE : SIDE + 1]
     left_rows(MIX, scale)
     product(0, tiles_s, to_left(1))
-    for dy in (0, -1, 1):
+
+    def mixed_middle(j, carry):
+        split_row(MIX, row_id(0, -1, 0) + j, tiles_p, scale)
+        return carry
+
+    def mixed_sides(j, carry):
+        skip = lax.rem(j + 1, 3) * TYPES
         for kind in range(TYPES):
-            split_row(MIX, row_id(0, dy, kind), tiles_p, scale)
-    for dy in (0, -1, 1):
-        for u in (1, -1):
-            for kind in range(TYPES):
-                row_copy(MIX, 0, dy, kind, -u, 0).wait_recv()
-                split_row(MIX, row_id(u, dy, kind), tiles_p, scale)
+            for u in (1, -1):
+                which = row_id(u, -1, kind) + skip
+                landed(MIX, which)
+                split_row(MIX, which, tiles_p, scale)
+        return carry
+
+    lax.fori_loop(0, 3 * TYPES, mixed_middle, 0)
+    lax.fori_loop(0, 3, mixed_sides, 0)
     product(1, tiles_p, to_left_and_second(0))
     product(0, tiles_s, to_left(1))
 
@@ -437,26 +459,25 @@
             band += folded((last[i, :, columns] * inverse) * ham_home[i, :, columns])
 
     def joined(sums):
-        sizes = sums[:, 2]
-        biggest = jnp.max(sizes, axis=0)
-        return jnp.sum(sums[:, 0], axis=0), jnp.sum(sums[:, 1] * (sizes / biggest[None]), axis=0), biggest
-
-    near_sums[1, at_low, 0] = count
-    near_sums[1, at_low, 1] = band
-    near_sums[1, at_low, 2] = jnp.broadcast_to(size, (8, 128))
+        biggest = jnp.max(sums, axis=0)
+        ratio = pltpu.roll(sums, SIDE, 2) / pltpu.roll(biggest, SIDE, 1)[None]
+        added = jnp.sum(jnp.where((across >= 32)[None], sums * ratio, sums), axis=0)
+        return jnp.where(across < SIDE, added, biggest)
+
+    near_sums[1, at_low] = jnp.where(
+        across < 32, over_all(count), jnp.where(across < SIDE, over_all(band), size)
+    )
     spread(near_copy, 1, at_low, group)
     collect(near_copy, 1, at_low, group)
-    part = joined(near_sums[1])
-    for k in range(3):
-        far_sums[1, at_high, k] = part[k]
+    far_sums[1, at_high] = joined(near_sums[1])
     spread(far_copy, 1, at_high, high)
     collect(far_copy, 1, at_high, high)
-    count, band, size = joined(far_sums[1])
-    scale = count_start / over_all(count)
+    sums = joined(far_sums[1])
+    scale = count_start / sums[:, :1]
     for slot in range(TYPES):
         out[0, 0, slot] = scale * last[near_s[4, TYPES, slot]]
     basis = nx * ny * TYPES * SIDE
-    energy[0] = jnp.sum(over_all(band * (size * scale))) / basis
+    energy[0] = jnp.sum(sums[:, 32:33] * (sums[:, SIDE : SIDE + 1] * scale)) / basis
 
     for copy in (*near_copies, *ham_copies, *flying.values()):
         copy.wait_send()
@@ -497,8 +518,8 @@
             pltpu.SMEM((9, 8, 128), I32),
             pltpu.VMEM((TYPES * KEPT, 128), I32),
             pltpu.SMEM((TYPES * KEPT, 128), I32),
-            pltpu.VMEM((2, group, 3, 8, 128), F32),
-            pltpu.VMEM((2, high, 3, 8, 128), F32),
+            pltpu.VMEM((2, group, 1, 128), F32),
+            pltpu.VMEM((2, high, 1, 128), F32),
             dma((3, 9 * TYPES)),
             dma((3, 9 * TYPES)),
             dma((TYPES,)),

time: 135 us -> 112 us (0.83)
  Pallas kernels: 128 us -> 105 us
    pallas_call x1, Pallas kernels: 128 us -> 105 us  [shards(): pl.pallas_call(functools.partial(kernel, nx, ny), out_shape=(jax.ShapeDty...]
where the time goes in v2:
time: 112 us
  Pallas kernels  105 us (94%)
  local copies, waits for them, and re-layouts  4.6 us (4%)
  between operations  2.49 us (2%)
    pallas_call x1, Pallas kernels, shards(): pl.pallas_call(functools.partial(kernel, nx, ny), out_shape=(jax.ShapeDty...  105 us
    unnamed x13, local copies, waits for them, and re-layouts  4.6 us

profile of v2, /device:TPU:1, one launch (start us, length us, event | category | flops | bytes accessed | tf_op | source)
XLA Modules:
  0.0 112.2 jit_solution(9931377438639911154)
XLA Ops:
  0.6 0.0 copy-start.4
  0.6 0.0 copy-start.3
  0.7 0.0 copy-start.5
  0.7 0.7 copy-done.4
  1.3 0.0 copy-done.3
  1.3 0.0 copy-done.5
  1.3 0.0 copy-start
  1.3 1.0 copy-done
  2.4 0.0 copy-start.1
  2.4 1.0 copy-done.1
  3.4 0.0 copy-start.2
  3.4 1.0 copy-done.2
  4.5 105.1 %shard_map.77 = (f32[1,1,4,64,512]{4,3,2,1,0:T(8,128)S(1)}, f32[1]{0:T(128)}) custom-call(f32[1,1,4,64,512]{4,3,2,1,0:T(8,128)S(1)} %copy-done, f32[1,1,4,64,512]{4,3,2,1,0:T(8,128)S(1)} %copy-done.1, f32[1,1,4,64,512]{4,3,2,1,0:T(8,128)S(1)} %copy-done.2, s32[4]{0:T(128)S(1)} %bitcast.6, s32[4,8]{1,0:T(4,128)S(1)} %bitcast.4, s32[4,8]{1,0:T(4,128)S(1)} %bitcast.5), custom_call_target="tpu_custom_call" | custom-call | tf_op jit(solution)/shard_map/pallas_call | solution.py:500
  109.5 0.8 copy.10
Async XLA Ops:
  0.6 0.7 copy-start.4
  0.6 0.7 copy-start.3
  0.7 0.7 copy-start.5
  1.3 1.0 copy-start
  2.4 1.0 copy-start.1
  3.4 1.0 copy-start.2

commit v3 on v2

--- a/solution.py
+++ b/solution.py
@@ -33,11 +33,12 @@
 
 def kernel(
     nx, ny,
+    ham_hbm, ovl_hbm, den_hbm, leaving_hbm, codes_hbm, slots_hbm,
+    out, energy,
     ham, ovl, den, leaving, codes, slots,
-    out, energy,
     rim, ham_out, ham_home, tiles_s, tiles_p, lhs, second, last,
     near, near_s, index_v, index_s, near_sums, far_sums,
-    send_sem, recv_sem, ham_send, ham_recv, near_send, near_recv, sum_send, sum_recv, local_sem,
+    send_sem, recv_sem, ham_send, ham_recv, near_send, near_recv, sum_send, sum_recv, local_sem, load_sem,
 ):
     x, y = lax.axis_index("gx"), lax.axis_index("gy")
     high = nx // LOW
@@ -53,6 +54,16 @@
     def far_peer(j):
         return (j * LOW + x % LOW, y)
 
+    loads = [
+        pltpu.make_async_copy(there, here, load_sem.at[k])
+        for k, (there, here) in enumerate((
+            (leaving_hbm, leaving), (codes_hbm, codes), (slots_hbm, slots),
+            (ovl_hbm, ovl), (den_hbm, den), (ham_hbm, ham),
+        ))
+    ]
+    for load in loads:
+        load.start()
+
     barrier = pltpu.get_barrier_semaphore()
     for ux, uy in AROUND:
         pl.semaphore_signal(barrier, inc=1, device_id=beside(ux, uy), device_id_type=MESH)
@@ -71,17 +82,8 @@
     lane = lax.broadcasted_iota(I32, (8, 128), 1)
     sub = lax.broadcasted_iota(I32, (8, 128), 0)
 
-    start = jnp.zeros((8, 128), F32)
-    for kind in range(TYPES):
-        slot = leaving[kind]
-        mine = row_id(*((1, 0), (-1, 0), (0, 1), (0, -1))[kind], kind)
-        s_row, p_row = ovl[0, 0, slot], den[0, 0, slot]
-        rim[OVL, mine] = s_row
-        rim[DEN, mine] = p_row
-        prod = s_row * p_row
-        for k in range(COLUMNS // 128):
-            start += folded(prod[:, k * 128 : (k + 1) * 128])
-
+    for load in loads[:3]:
+        load.wait()
     note = jnp.zeros((8, 128), I32)
     for kind in range(TYPES):
         slot = leaving[BEHIND[kind]]
@@ -91,34 +93,65 @@
         note = jnp.where((sub == TYPES) & (lane == slot), kind, note)
     near[4] = note
 
+    for load in loads[3:5]:
+        load.wait()
+    start = jnp.zeros((8, 128), F32)
+    for kind in range(TYPES):
+        slot = leaving[kind]
+        mine = row_id(*((1, 0), (-1, 0), (0, 1), (0, -1))[kind], kind)
+        s_row, p_row = ovl[slot], den[slot]
+        rim[OVL, mine] = s_row
+        rim[DEN, mine] = p_row
+        prod = s_row * p_row
+        for k in range(COLUMNS // 128):
+            start += folded(prod[:, k * 128 : (k + 1) * 128])
+
     pl.semaphore_wait(barrier, len(AROUND) + group - 1 + high - 1)
 
-    def row_copy(m, dx, dy, kind, ux, uy):
-        there = row_id(dx - ux, dy - uy, kind)
+    def row_copy(m, which, there, ux, uy, left=None):
         return pltpu.make_async_remote_copy(
-            src_ref=rim.at[m, row_id(dx, dy, kind)],
+            src_ref=rim.at[m, which],
             dst_ref=rim.at[m, there],
-            send_sem=send_sem.at[m, there],
+            send_sem=send_sem.at[m, there if left is None else left],
             recv_sem=recv_sem.at[m, there],
             device_id=beside(ux, uy),
             device_id_type=MESH,
         )
 
-    flying = {}
-
     def send(m, dx, dy, kind, ux, uy):
-        copy = row_copy(m, dx, dy, kind, ux, uy)
-        copy.start()
-        flying[m, dx - ux, dy - uy, kind] = copy
-
-    def initial(m):
+        row_copy(m, row_id(dx, dy, kind), row_id(dx - ux, dy - uy, kind), ux, uy).start()
+
+    def landed(m, which):
+        row_copy(m, which, which, 1, 0).wait_recv()
+
+    def arrive(m, dx, dy, kind):
+        landed(m, row_id(dx, dy, kind))
+
+    core = lax.rem(x, 2)
+    outer, inner = 2 * core - 1, 1 - 2 * core
+    outer_ids, inner_ids = core * (6 * TYPES), (1 - core) * (6 * TYPES)
+
+    def outer_id(dy, kind):
+        return outer_ids + ((dy + 1) * TYPES + kind)
+
+    def send_inner(m, dy, kind):
+        left = inner_ids + ((dy + 1) * TYPES + kind)
+        row_copy(m, row_id(0, dy, kind), outer_id(dy, kind), inner, 0, left).start()
+
+    def outer_on(m, dy, kind, uy):
+        landed(m, outer_id(dy, kind))
+        row_copy(m, outer_id(dy, kind), outer_id(dy - uy, kind), 0, uy).start()
+
+    def start_y(m):
         send(m, 0, 1, C, 0, 1)
         send(m, 0, -1, D, 0, -1)
-        send(m, 1, 0, A, 1, 0)
-        send(m, -1, 0, B, -1, 0)
         for u in (1, -1):
             send(m, 1, 0, A, 0, u)
             send(m, -1, 0, B, 0, u)
+
+    def start_x(m):
+        send(m, 1, 0, A, 1, 0)
+        send(m, -1, 0, B, -1, 0)
         for u in (1, -1):
             send(m, 0, 1, C, u, 0)
             send(m, 0, -1, D, u, 0)
@@ -140,21 +173,19 @@
             near_copies.append(copy)
 
     tell_pattern()
-    initial(OVL)
-    initial(DEN)
-
-    def arrive(m, dx, dy, kind):
-        flying[m, dx, dy, kind].wait_recv()
+    start_y(OVL)
+    start_x(OVL)
+    start_x(DEN)
 
     def first_tier(m):
-        arrive(m, 0, 0, C)
-        send(m, 0, 0, C, 0, 1)
-        for u in (1, -1):
-            send(m, 0, 0, C, u, 0)
-        arrive(m, 0, 0, D)
-        send(m, 0, 0, D, 0, -1)
-        for u in (1, -1):
-            send(m, 0, 0, D, u, 0)
+        for kind, uy in ((C, 1), (D, -1)):
+            arrive(m, 0, 0, kind)
+            send(m, 0, 0, kind, 0, uy)
+            if m == OVL:
+                for u in (1, -1):
+                    send(m, 0, 0, kind, u, 0)
+            else:
+                send_inner(m, 0, kind)
         arrive(m, 0, 0, A)
         send(m, 0, 0, A, 1, 0)
         arrive(m, 0, 0, B)
@@ -164,14 +195,18 @@
             send(m, 1, u, A, 1, 0)
             arrive(m, -1, u, B)
             send(m, -1, u, B, -1, 0)
+        if m == DEN:
+            outer_on(m, 0, C, 1)
+            outer_on(m, 0, D, -1)
 
     def second_tier(m):
-        arrive(m, 0, -1, C)
-        for u in (1, -1):
-            send(m, 0, -1, C, u, 0)
-        arrive(m, 0, 1, D)
-        for u in (1, -1):
-            send(m, 0, 1, D, u, 0)
+        for kind, uy in ((C, 1), (D, -1)):
+            arrive(m, 0, -uy, kind)
+            if m == OVL:
+                for u in (1, -1):
+                    send(m, 0, -uy, kind, u, 0)
+            else:
+                send_inner(m, -uy, kind)
         for u in (1, -1):
             arrive(m, 0, u, A)
             send(m, 0, u, A, 1, 0)
@@ -252,6 +287,9 @@
     to_scalars.wait()
 
     first_tier(OVL)
+    start_y(DEN)
+    outer_on(DEN, 1, C, 1)
+    outer_on(DEN, -1, D, -1)
 
     for kind in range(TYPES):
         slot = leaving[BEHIND[kind]]
@@ -275,16 +313,6 @@
     first_tier(DEN)
     left_rows(DEN)
 
-    def landed(m, which):
-        pltpu.make_async_remote_copy(
-            src_ref=rim.at[m, which],
-            dst_ref=rim.at[m, which],
-            send_sem=send_sem.at[m, which],
-            recv_sem=recv_sem.at[m, which],
-            device_id=beside(1, 0),
-            device_id_type=MESH,
-        ).wait_recv()
-
     def middle(m, tiles):
         def one(j, carry):
             split_row(m, row_id(0, -1, 0) + j, tiles)
@@ -301,10 +329,23 @@
     def third_tier(m, tiles):
         def one(j, carry):
             skip = lax.rem(j + 1, 3) * TYPES
+            if m == DEN:
+                for kind in (C, D):
+                    landed(m, inner_ids + kind + skip)
+
+                @pl.when(j == 1)
+                def _():
+                    landed(m, outer_id(1, D))
+
+                @pl.when(j == 2)
+                def _():
+                    landed(m, outer_id(-1, C))
+
             for u, kinds in ((1, (B, C, D)), (-1, (A, C, D))):
                 for kind in kinds:
                     which = row_id(u, -1, kind) + skip
-                    landed(m, which)
+                    if m == OVL or kind < C:
+                        landed(m, which)
                     split_row(m, which, tiles)
             return carry
 
@@ -315,8 +356,9 @@
     second_tier(DEN)
 
     ham_copies = []
+    loads[5].wait()
     for kind in range(TYPES):
-        ham_out[kind] = ham[0, 0, leaving[kind]]
+        ham_out[kind] = ham[leaving[kind]]
     for kind, (ux, uy) in enumerate(((1, 0), (-1, 0), (0, 1), (0, -1))):
         copy = pltpu.make_async_remote_copy(
             src_ref=ham_out.at[kind],
@@ -340,9 +382,17 @@
         rim[MIX, own + i, :, columns] = m
         return total + folded(m * rim[OVL, own + i, :, columns])
 
+    def mixed_along_y(i):
+        for u in (1, -1):
+            row_copy(MIX, own + i, row_id(0, -u, 0) + i, 0, u).start()
+
     def mixed_sent(i):
-        for ux, uy in ((0, 1), (0, -1), (1, 0), (-1, 0)):
-            row_copy(MIX, 0, 0, i, ux, uy).start()
+        for u in (1, -1):
+            row_copy(MIX, own + i, row_id(-u, 0, 0) + i, u, 0).start()
+
+        @pl.when(i < 2)
+        def _():
+            mixed_along_y(i)
 
     count = product(1, tiles_p, mixed_out, mixed_sent, jnp.zeros((8, 128), F32))
 
@@ -396,26 +446,32 @@
     near_sums[0, at_low] = jnp.where(across < SIDE, over_all(start), over_all(count))
     spread(near_copy, 0, at_low, group)
 
-
     def pass_on(i):
         for dy in (-1, 1):
-            row_copy(MIX, 0, 0, i, 0, -dy).wait_recv()
+            arrive(MIX, 0, dy, i)
             for u in (1, -1):
-                row_copy(MIX, 0, dy, i, u, 0).start()
-
-    pass_on(0)
+                send(MIX, 0, dy, i, u, 0)
+
     collect(near_copy, 0, at_low, group)
     far_sums[0, at_high] = jnp.sum(near_sums[0], axis=0)
     spread(far_copy, 0, at_high, high)
+    pass_on(0)
     pass_on(1)
-    pass_on(2)
-    pass_on(3)
+    mixed_along_y(2)
+    for u in (1, -1):
+        if u == 1:
+            landed(MIX, outer_id(0, 3))
+        row_copy(MIX, outer_id(0, 3), outer_id(-u, 3), 0, u).start()
+    mixed_along_y(3)
     collect(far_copy, 0, at_high, high)
-
     counts = jnp.sum(far_sums[0], axis=0)
     count_start = counts[:, :1]
     scale = count_start / counts[:, SIDE : SIDE + 1]
     left_rows(MIX, scale)
+    pass_on(2)
+    for dy in (-1, 1):
+        arrive(MIX, 0, dy, 3)
+        send_inner(MIX, dy, 3)
     product(0, tiles_s, to_left(1))
 
     def mixed_middle(j, carry):
@@ -424,10 +480,17 @@
 
     def mixed_sides(j, carry):
         skip = lax.rem(j + 1, 3) * TYPES
+        landed(MIX, inner_ids + 3 + skip)
+
+        @pl.when(j > 0)
+        def _():
+            landed(MIX, outer_ids + 3 + skip)
+
         for kind in range(TYPES):
             for u in (1, -1):
                 which = row_id(u, -1, kind) + skip
-                landed(MIX, which)
+                if kind < 3:
+                    landed(MIX, which)
                 split_row(MIX, which, tiles_p, scale)
         return carry
 
@@ -479,14 +542,15 @@
     basis = nx * ny * TYPES * SIDE
     energy[0] = jnp.sum(sums[:, 32:33] * (sums[:, SIDE : SIDE + 1] * scale)) / basis
 
-    for copy in (*near_copies, *ham_copies, *flying.values()):
+    for copy in (*near_copies, *ham_copies):
         copy.wait_send()
-    for i in range(TYPES):
-        for ux, uy in ((0, 1), (0, -1), (1, 0), (-1, 0)):
-            row_copy(MIX, 0, 0, i, ux, uy).wait_send()
-        for dy in (-1, 1):
-            for u in (1, -1):
-                row_copy(MIX, 0, dy, i, u, 0).wait_send()
+
+    first = {OVL: (row_id(1, 0, A), row_id(-1, 0, B), row_id(0, 1, C), row_id(0, -1, D))}
+    first[DEN], first[MIX] = first[OVL], tuple(own + i for i in range(TYPES))
+    for m in (OVL, DEN, MIX):
+        for which in range(9 * TYPES):
+            if which not in first[m]:
+                row_copy(m, which, which, 1, 0).wait_send()
     for s in range(2):
         sent(near_copy, s, at_low, group)
         sent(far_copy, s, at_high, high)
@@ -503,9 +567,13 @@
             jax.ShapeDtypeStruct(den.shape, F32),
             jax.ShapeDtypeStruct((1,), F32),
         ),
-        in_specs=[vmem] * 3 + [smem] * 3,
+        in_specs=[pl.BlockSpec(memory_space=pl.ANY)] * 6,
         out_specs=(vmem, smem),
         scratch_shapes=[
+            *[pltpu.VMEM((TYPES, SIDE, COLUMNS), F32)] * 3,
+            pltpu.SMEM((TYPES,), I32),
+            pltpu.SMEM((TYPES, KEPT), I32),
+            pltpu.SMEM((TYPES, KEPT), I32),
             pltpu.VMEM((3, 9 * TYPES, SIDE, COLUMNS), F32),
             pltpu.VMEM((TYPES, SIDE, COLUMNS), F32),
             pltpu.VMEM((TYPES, SIDE, COLUMNS), F32),
@@ -529,12 +597,13 @@
             dma((2, 2, max(group, high))),
             dma((2, 2, max(group, high))),
             dma((2,)),
+            dma((6,)),
         ],
         compiler_params=pltpu.CompilerParams(
-            collective_id=0, has_side_effects=True, vmem_limit_bytes=48 * 1024 * 1024
+            collective_id=0, has_side_effects=True, vmem_limit_bytes=60 * 1024 * 1024
         ),
     )(
-        ham, ovl, den,
+        *(m.reshape(TYPES, SIDE, COLUMNS) for m in (ham, ovl, den)),
         leaving.reshape(TYPES), codes.reshape(TYPES, KEPT), slots.reshape(TYPES, KEPT),
     )
     return purified, energy.reshape(())

time: 112 us -> 96.9 us (0.87)
  Pallas kernels: 105 us -> 92.5 us
  local copies, waits for them, and re-layouts: 4.6 us -> 1.87 us
    pallas_call x1, Pallas kernels: 105 us -> 92.5 us  [shards(): pl.pallas_call(functools.partial(kernel, nx, ny), out_shape=(jax.ShapeDty...]
    unnamed x13 -> x1, local copies, waits for them, and re-layouts: 4.6 us -> 1.87 us
where the time goes in v3:
time: 96.9 us; the launch traced here: 96.7 us
  Pallas kernels  92.5 us (95%)
  between operations  2.34 us (2%)
  local copies, waits for them, and re-layouts  1.87 us (2%)
    pallas_call x1, Pallas kernels, shards(): pl.pallas_call(functools.partial(kernel, nx, ny), out_shape=(jax.ShapeDty...  92.5 us

profile of v3, /device:TPU:1, one launch (start us, length us, event | category | flops | bytes accessed | tf_op | source)
XLA Modules:
  0.0 96.7 jit_solution(12775727150640663459)
XLA Ops:
  0.6 92.5 %shard_map.77 = (f32[1,1,4,64,512]{4,3,2,1,0:T(8,128)}, f32[1]{0:T(128)}) custom-call(f32[4,64,512]{2,1,0:T(8,128)} %bitcast.7, f32[4,64,512]{2,1,0:T(8,128)} %bitcast.8, f32[4,64,512]{2,1,0:T(8,128)} %bitcast.9, s32[4]{0:T(128)} %bitcast.12, s32[4,8]{1,0:T(4,128)} %bitcast.10, s32[4,8]{1,0:T(4,128)} %bitcast.11), custom_call_target="tpu_custom_call" | custom-call | tf_op jit(solution)/shard_map/pallas_call | solution.py:564
  93.1 1.9 %copy.10 = f32[1,1,4,64,512]{4,3,2,1,0:T(8,128)} copy(f32[1,1,4,64,512]{4,3,2,1,0:T(8,128)} %get-tuple-element.8) | data formatting | bytes 1048576

commit v4 on v3

--- a/solution.py
+++ b/solution.py
@@ -237,28 +237,26 @@
 
     wide = lax.broadcasted_iota(I32, (SIDE, 128), 1) < SIDE
 
-    def product(left, tiles, emit, after=None, carry=0):
-        def one_row(i, carry):
-            a = lhs[left, i]
-            for pair in range(KEPT // 2):
-                right = jnp.concatenate(
-                    [
-                        jnp.concatenate([tiles[index_s[i * KEPT + b, e]] for e in range(KEPT)], axis=0)
-                        for b in (2 * pair, 2 * pair + 1)
-                    ],
-                    axis=1,
-                )
-                full = jnp.dot(a, right, preferred_element_type=F32)
-                both = full[:SIDE] + full[SIDE:]
-                even, odd = both[:, :128], both[:, 128:]
-                even = even + pltpu.roll(even, SIDE, 1)
-                odd = odd + pltpu.roll(odd, SIDE, 1)
-                carry = emit(i, slice(pair * 128, (pair + 1) * 128), jnp.where(wide, even, odd), carry)
-            if after is not None:
-                after(i)
-            return carry
-
-        return lax.fori_loop(0, TYPES, one_row, carry)
+    def row_product(left, tiles, i, emit, carry=0):
+        a = lhs[left, i]
+        for pair in range(KEPT // 2):
+            right = jnp.concatenate(
+                [
+                    jnp.concatenate([tiles[index_s[i * KEPT + b, e]] for e in range(KEPT)], axis=0)
+                    for b in (2 * pair, 2 * pair + 1)
+                ],
+                axis=1,
+            )
+            full = jnp.dot(a, right, preferred_element_type=F32)
+            both = full[:SIDE] + full[SIDE:]
+            even, odd = both[:, :128], both[:, 128:]
+            even = even + pltpu.roll(even, SIDE, 1)
+            odd = odd + pltpu.roll(odd, SIDE, 1)
+            carry = emit(i, slice(pair * 128, (pair + 1) * 128), jnp.where(wide, even, odd), carry)
+        return carry
+
+    def product(left, tiles, emit, carry=0):
+        return lax.fori_loop(0, TYPES, lambda i, carry: row_product(left, tiles, i, emit, carry), carry)
 
     def to_left(into):
         def emit(i, columns, v, carry):
@@ -280,16 +278,16 @@
     for k in range(KEPT):
         tiles_s[k] = jnp.zeros((SIDE, 128), BF16)
         tiles_p[k] = jnp.zeros((SIDE, 128), BF16)
+    first_tier(OVL)
+    start_y(DEN)
+    outer_on(DEN, 1, C, 1)
+    outer_on(DEN, -1, D, -1)
+
     for copy in near_copies:
         copy.wait_recv()
     to_scalars = pltpu.make_async_copy(near, near_s, local_sem.at[0])
     to_scalars.start()
     to_scalars.wait()
-
-    first_tier(OVL)
-    start_y(DEN)
-    outer_on(DEN, 1, C, 1)
-    outer_on(DEN, -1, D, -1)
 
     for kind in range(TYPES):
         slot = leaving[BEHIND[kind]]
@@ -374,8 +372,6 @@
     product(0, tiles_s, to_left(1))
     middle(DEN, tiles_p)
     third_tier(DEN, tiles_p)
-    product(1, tiles_p, to_left_and_second(0))
-    product(0, tiles_s, to_left(1))
 
     def mixed_out(i, columns, v, total):
         m = 3.0 * second[i, :, columns] - 2.0 * v
@@ -394,7 +390,14 @@
         def _():
             mixed_along_y(i)
 
-    count = product(1, tiles_p, mixed_out, mixed_sent, jnp.zeros((8, 128), F32))
+    def one_row(i, total):
+        row_product(1, tiles_p, i, to_left_and_second(0))
+        row_product(0, tiles_s, i, to_left(1))
+        total = row_product(1, tiles_p, i, mixed_out, total)
+        mixed_sent(i)
+        return total
+
+    count = lax.fori_loop(0, TYPES, one_row, jnp.zeros((8, 128), F32))
 
     def near_copy(s, j, mine):
         return pltpu.make_async_remote_copy(
@@ -421,7 +424,7 @@
             copy_of(s, (me + o) % members, me).start()
             return carry
 
-        lax.fori_loop(1, members, step, 0)
+        lax.fori_loop(1, members, step, 0, unroll=True)
 
     def collect(copy_of, s, me, members):
         def step(o, carry):
@@ -429,7 +432,7 @@
             copy_of(s, j, j).wait_recv()
             return carry
 
-        lax.fori_loop(1, members, step, 0)
+        lax.fori_loop(1, members, step, 0, unroll=True)
 
     def sent(copy_of, s, me, members):
         def step(o, carry):
@@ -452,23 +455,23 @@
             for u in (1, -1):
                 send(MIX, 0, dy, i, u, 0)
 
+    pass_on(0)
+    mixed_along_y(2)
     collect(near_copy, 0, at_low, group)
     far_sums[0, at_high] = jnp.sum(near_sums[0], axis=0)
     spread(far_copy, 0, at_high, high)
-    pass_on(0)
     pass_on(1)
-    mixed_along_y(2)
+    mixed_along_y(3)
+    pass_on(2)
     for u in (1, -1):
         if u == 1:
             landed(MIX, outer_id(0, 3))
         row_copy(MIX, outer_id(0, 3), outer_id(-u, 3), 0, u).start()
-    mixed_along_y(3)
     collect(far_copy, 0, at_high, high)
     counts = jnp.sum(far_sums[0], axis=0)
     count_start = counts[:, :1]
     scale = count_start / counts[:, SIDE : SIDE + 1]
     left_rows(MIX, scale)
-    pass_on(2)
     for dy in (-1, 1):
         arrive(MIX, 0, dy, 3)
         send_inner(MIX, dy, 3)
@@ -509,7 +512,7 @@
         )
 
     zero = jnp.zeros((8, 128), F32)
-    count, largest = product(1, tiles_p, last_out, None, (zero, zero))
+    count, largest = product(1, tiles_p, last_out, (zero, zero))
     for copy in ham_copies:
         copy.wait_recv()
     largest = jnp.max(jnp.max(largest, axis=1, keepdims=True), axis=0, keepdims=True)
@@ -531,6 +534,17 @@
         across < 32, over_all(count), jnp.where(across < SIDE, over_all(band), size)
     )
     spread(near_copy, 1, at_low, group)
+    for copy in (*near_copies, *ham_copies):
+        copy.wait_send()
+
+    first = {OVL: (row_id(1, 0, A), row_id(-1, 0, B), row_id(0, 1, C), row_id(0, -1, D))}
+    first[DEN], first[MIX] = first[OVL], tuple(own + i for i in range(TYPES))
+    for m in (OVL, DEN, MIX):
+        for which in range(9 * TYPES):
+            if which not in first[m]:
+                row_copy(m, which, which, 1, 0).wait_send()
+    sent(near_copy, 0, at_low, group)
+    sent(far_copy, 0, at_high, high)
     collect(near_copy, 1, at_low, group)
     far_sums[1, at_high] = joined(near_sums[1])
     spread(far_copy, 1, at_high, high)
@@ -542,18 +556,8 @@
     basis = nx * ny * TYPES * SIDE
     energy[0] = jnp.sum(sums[:, 32:33] * (sums[:, SIDE : SIDE + 1] * scale)) / basis
 
-    for copy in (*near_copies, *ham_copies):
-        copy.wait_send()
-
-    first = {OVL: (row_id(1, 0, A), row_id(-1, 0, B), row_id(0, 1, C), row_id(0, -1, D))}
-    first[DEN], first[MIX] = first[OVL], tuple(own + i for i in range(TYPES))
-    for m in (OVL, DEN, MIX):
-        for which in range(9 * TYPES):
-            if which not in first[m]:
-                row_copy(m, which, which, 1, 0).wait_send()
-    for s in range(2):
-        sent(near_copy, s, at_low, group)
-        sent(far_copy, s, at_high, high)
+    sent(near_copy, 1, at_low, group)
+    sent(far_copy, 1, at_high, high)
 
 
 def shards(nx, ny, ham, ovl, den, leaving, codes, slots):

time: 96.9 us -> 90.5 us (0.934)
  Pallas kernels: 92.5 us -> 86.1 us
    pallas_call x1, Pallas kernels: 92.5 us -> 86.1 us  [shards(): pl.pallas_call(functools.partial(kernel, nx, ny), out_shape=(jax.ShapeDty...]
where the time goes in v4:
time: 90.5 us; the launch traced here: 90.3 us
  Pallas kernels  86.1 us (95%)
  between operations  2.34 us (3%)
  local copies, waits for them, and re-layouts  1.87 us (2%)
    pallas_call x1, Pallas kernels, shards(): pl.pallas_call(functools.partial(kernel, nx, ny), out_shape=(jax.ShapeDty...  86.1 us
    unnamed x1, local copies, waits for them, and re-layouts  1.87 us

profile of v4, /device:TPU:1, one launch (start us, length us, event | category | flops | bytes accessed | tf_op | source)
XLA Modules:
  0.0 90.3 jit_solution(12090219424435526487)
XLA Ops:
  0.6 86.1 %shard_map.77 = (f32[1,1,4,64,512]{4,3,2,1,0:T(8,128)}, f32[1]{0:T(128)}) custom-call(f32[4,64,512]{2,1,0:T(8,128)} %bitcast.7, f32[4,64,512]{2,1,0:T(8,128)} %bitcast.8, f32[4,64,512]{2,1,0:T(8,128)} %bitcast.9, s32[4]{0:T(128)} %bitcast.12, s32[4,8]{1,0:T(4,128)} %bitcast.10, s32[4,8]{1,0:T(4,128)} %bitcast.11), custom_call_target="tpu_custom_call" | custom-call | tf_op jit(solution)/shard_map/pallas_call | solution.py:568
  86.8 1.9 %copy.10 = f32[1,1,4,64,512]{4,3,2,1,0:T(8,128)} copy(f32[1,1,4,64,512]{4,3,2,1,0:T(8,128)} %get-tuple-element.8) | data formatting | bytes 1048576

commit v5 on v4

--- a/solution.py
+++ b/solution.py
@@ -173,8 +173,8 @@
             near_copies.append(copy)
 
     tell_pattern()
+    start_x(OVL)
     start_y(OVL)
-    start_x(OVL)
     start_x(DEN)
 
     def first_tier(m):
@@ -256,7 +256,7 @@
         return carry
 
     def product(left, tiles, emit, carry=0):
-        return lax.fori_loop(0, TYPES, lambda i, carry: row_product(left, tiles, i, emit, carry), carry)
+        return lax.fori_loop(0, TYPES, lambda i, carry: row_product(left, tiles, i, emit, carry), carry, unroll=True)
 
     def to_left(into):
         def emit(i, columns, v, carry):

time: 90.5 us -> 87.1 us (0.962)
  Pallas kernels: 86.1 us -> 82.7 us
    pallas_call x1, Pallas kernels: 86.1 us -> 82.7 us  [shards(): pl.pallas_call(functools.partial(kernel, nx, ny), out_shape=(jax.ShapeDty...]
where the time goes in v5:
time: 87.1 us; the launch traced here: 87 us
  Pallas kernels  82.7 us (95%)
  between operations  2.34 us (3%)
  local copies, waits for them, and re-layouts  1.87 us (2%)
    pallas_call x1, Pallas kernels, shards(): pl.pallas_call(functools.partial(kernel, nx, ny), out_shape=(jax.ShapeDty...  82.7 us
    unnamed x1, local copies, waits for them, and re-layouts  1.87 us

profile of v5, /device:TPU:1, one launch (start us, length us, event | category | flops | bytes accessed | tf_op | source)
XLA Modules:
  0.0 87.0 jit_solution(10553369241557879462)
XLA Ops:
  0.6 82.7 %shard_map.77 = (f32[1,1,4,64,512]{4,3,2,1,0:T(8,128)}, f32[1]{0:T(128)}) custom-call(f32[4,64,512]{2,1,0:T(8,128)} %bitcast.7, f32[4,64,512]{2,1,0:T(8,128)} %bitcast.8, f32[4,64,512]{2,1,0:T(8,128)} %bitcast.9, s32[4]{0:T(128)} %bitcast.12, s32[4,8]{1,0:T(4,128)} %bitcast.10, s32[4,8]{1,0:T(4,128)} %bitcast.11), custom_call_target="tpu_custom_call" | custom-call | tf_op jit(solution)/shard_map/pallas_call | solution.py:568
  83.4 1.9 %copy.10 = f32[1,1,4,64,512]{4,3,2,1,0:T(8,128)} copy(f32[1,1,4,64,512]{4,3,2,1,0:T(8,128)} %get-tuple-element.8) | data formatting | bytes 1048576

commit v6 on v5

--- a/solution.py
+++ b/solution.py
@@ -497,8 +497,8 @@
                 split_row(MIX, which, tiles_p, scale)
         return carry
 
-    lax.fori_loop(0, 3 * TYPES, mixed_middle, 0)
-    lax.fori_loop(0, 3, mixed_sides, 0)
+    lax.fori_loop(0, 3 * TYPES, mixed_middle, 0, unroll=3)
+    lax.fori_loop(0, 3, mixed_sides, 0, unroll=True)
     product(1, tiles_p, to_left_and_second(0))
     product(0, tiles_s, to_left(1))
 
@@ -545,6 +545,7 @@
                 row_copy(m, which, which, 1, 0).wait_send()
     sent(near_copy, 0, at_low, group)
     sent(far_copy, 0, at_high, high)
+    sent(near_copy, 1, at_low, group)
     collect(near_copy, 1, at_low, group)
     far_sums[1, at_high] = joined(near_sums[1])
     spread(far_copy, 1, at_high, high)
@@ -556,7 +557,6 @@
     basis = nx * ny * TYPES * SIDE
     energy[0] = jnp.sum(sums[:, 32:33] * (sums[:, SIDE : SIDE + 1] * scale)) / basis
 
-    sent(near_copy, 1, at_low, group)
     sent(far_copy, 1, at_high, high)
 
 

time: 87.1 us -> 86.3 us (level)
  no operation moved by 1% of the time
where the time goes in v6:
time: 86.3 us; the launch traced here: 86.2 us
  Pallas kernels  82 us (95%)
  between operations  2.34 us (3%)
  local copies, waits for them, and re-layouts  1.87 us (2%)
    pallas_call x1, Pallas kernels, shards(): pl.pallas_call(functools.partial(kernel, nx, ny), out_shape=(jax.ShapeDty...  82 us
    unnamed x1, local copies, waits for them, and re-layouts  1.87 us

profile of v6, /device:TPU:1, one launch (start us, length us, event | category | flops | bytes accessed | tf_op | source)
XLA Modules:
  0.0 86.2 jit_solution(14943002789348622862)
XLA Ops:
  0.6 82.0 %shard_map.77 = (f32[1,1,4,64,512]{4,3,2,1,0:T(8,128)}, f32[1]{0:T(128)}) custom-call(f32[4,64,512]{2,1,0:T(8,128)} %bitcast.7, f32[4,64,512]{2,1,0:T(8,128)} %bitcast.8, f32[4,64,512]{2,1,0:T(8,128)} %bitcast.9, s32[4]{0:T(128)} %bitcast.12, s32[4,8]{1,0:T(4,128)} %bitcast.10, s32[4,8]{1,0:T(4,128)} %bitcast.11), custom_call_target="tpu_custom_call" | custom-call | tf_op jit(solution)/shard_map/pallas_call | solution.py:568
  82.6 1.9 %copy.10 = f32[1,1,4,64,512]{4,3,2,1,0:T(8,128)} copy(f32[1,1,4,64,512]{4,3,2,1,0:T(8,128)} %get-tuple-element.8) | data formatting | bytes 1048576
